TPU v7x, 128 devices: a whole 4x4x4 slice. The times are simulated.
128 devices in a mesh: seq: 64 (over z_lo, y, x, core), grp: 2 (over z_hi).
Axes of the slice: x: 4, y: 4, z: 4 (z_hi: 2, z_lo: 2; z = z_hi * 2 + z_lo), core: 2. Of those that a mesh axis runs over, the one named last changes fastest.
Arguments:
- inputs: bfloat16 [8192, 2048], P('seq'), may hold values from -16 to 16
- attention_gain: float32 [2048], replicated, may hold values from 0.25 to 1.75
- query_weight: bfloat16 [2048, 2048], P('seq', 'grp'), may hold values from -0.125 to 0.125
- key_matrix: bfloat16 [2048, 1024], P('seq', 'grp'), may hold values from -0.125 to 0.125
- value_matrix: bfloat16 [2048, 1024], P('seq', 'grp'), may hold values from -0.125 to 0.125
- gate_weight: bfloat16 [2048, 16], P('seq', 'grp'), may hold values from -0.125 to 0.125
- query_gain: float32 [128], replicated, may hold values from 0.25 to 1.75
- key_gain: float32 [128], replicated, may hold values from 0.25 to 1.75
- out_weight: bfloat16 [2048, 2048], P('grp', 'seq'), may hold values from -3 to 3
- feed_gain: float32 [2048], replicated, may hold values from 0.25 to 1.75
- feed_gate: bfloat16 [2048, 6144], P('seq', 'grp'), may hold values from -0.125 to 0.125
- feed_up: bfloat16 [2048, 6144], P('seq', 'grp'), may hold values from -0.125 to 0.125
- feed_down: bfloat16 [6144, 2048], P('grp', 'seq'), may hold values from -0.078125 to 0.078125
- cotangent: bfloat16 [8192, 2048], P('seq'), may hold values from -16 to 16
Outputs:
- output: bfloat16 [8192, 2048], P('seq')
- grad_inputs: bfloat16 [8192, 2048], P('seq')
- grad_attention_gain: float32 [2048], P('seq')
- grad_query_weight: float32 [2048, 2048], P('seq', 'grp')
- grad_key_weight: float32 [2048, 1024], P('seq', 'grp')
- grad_value_weight: float32 [2048, 1024], P('seq', 'grp')
- grad_gate_weight: float32 [2048, 16], P('seq', 'grp')
- grad_query_gain: float32 [128], replicated
- grad_key_gain: float32 [128], replicated
- grad_out_weight: float32 [2048, 2048], P('grp', 'seq')
- grad_feed_gain: float32 [2048], P('seq')
- grad_feed_gate: float32 [2048, 6144], P('seq', 'grp')
- grad_feed_up: float32 [2048, 6144], P('seq', 'grp')
- grad_feed_down: float32 [6144, 2048], P('grp', 'seq')
All inputs are finite; a program needn't handle non-finite values.
Results may differ from a plain program's by a relative error of at most 0.022.
Values may be sent and summed in bfloat16 or wider, within the bound.
A program may use at most 256 MiB of HBM per device.

v0:
```python
from functools import partial

import jax
import jax.numpy as jnp
from jax import lax
from jax.sharding import PartitionSpec as P

EPSILON = 1e-06
ROPE_BASE = 1000000.0


def rms_norm(matrix, norm_gain):
    return (
        matrix * lax.rsqrt(jnp.mean(matrix * matrix, axis=-1, keepdims=True) + EPSILON) * norm_gain
    )


def rotate_half(head_rows, cosine_rows, sine_rows):
    middle = head_rows.shape[-1] // 2
    first_half = head_rows[..., :middle]
    second_half = head_rows[..., middle:]
    return jnp.concatenate(
        [
            first_half * cosine_rows - second_half * sine_rows,
            second_half * cosine_rows + first_half * sine_rows,
        ],
        axis=-1,
    )


def rope_tables(positions, head_size):
    middle = head_size // 2
    inverse = ROPE_BASE ** (-(jnp.arange(middle, dtype=jnp.float32) * 2.0) / head_size)
    angles = positions.astype(jnp.float32)[:, None] * inverse[None, :]
    return (jnp.cos(angles)[:, None, :], jnp.sin(angles)[:, None, :])


def head_prepare(projected, norm_gain, cosine_rows, sine_rows):
    return rotate_half(rms_norm(projected, norm_gain), cosine_rows, sine_rows)


def matmul(left_side, right_side):
    return jnp.dot(left_side, right_side, preferred_element_type=jnp.float32)


def inner(left_side, right_side):
    return lax.dot_general(
        left_side, right_side, (((0,), (0,)), ((), ())), preferred_element_type=jnp.float32
    )


def outer(left_side, right_side):
    return lax.dot_general(
        left_side, right_side, (((1,), (1,)), ((), ())), preferred_element_type=jnp.float32
    )


def swiglu(gate_part, up_part):
    return jax.nn.silu(gate_part) * up_part


def apply_gate(attended, gate_logits):
    return attended * jax.nn.sigmoid(gate_logits)[:, :, None]


def per_device(
    inputs,
    attention_gain,
    query_weight,
    key_matrix,
    value_matrix,
    gate_weight,
    query_gain,
    key_gain,
    out_weight,
    feed_gain,
    feed_gate,
    feed_up,
    feed_down,
    cotangent,
):
    row_count = inputs.shape[0]
    head_size = query_gain.shape[0]
    seq_devices = lax.axis_size("seq")
    seq_place = lax.axis_index("seq")
    total_rows = row_count * seq_devices
    block_length = min(512, total_rows)
    scale_factor = head_size ** (-0.5)
    full_query, full_key, full_value, full_gate, full_out = (
        lax.all_gather(query_weight, "seq", axis=0, tiled=True),
        lax.all_gather(key_matrix, "seq", axis=0, tiled=True),
        lax.all_gather(value_matrix, "seq", axis=0, tiled=True),
        lax.all_gather(gate_weight, "seq", axis=0, tiled=True),
        lax.all_gather(out_weight, "seq", axis=1, tiled=True),
    )
    query_heads = full_query.shape[1] // head_size
    key_heads = full_key.shape[1] // head_size
    group_width = query_heads // key_heads
    key_width = key_heads * head_size
    input_rows = inputs.astype(jnp.float32)
    normed_value, attention_norm_pull = jax.vjp(rms_norm, input_rows, attention_gain)
    normed_input = normed_value.astype(jnp.bfloat16)
    positions = seq_place * row_count + jnp.arange(row_count, dtype=jnp.int32)
    cosine_rows, sine_rows = rope_tables(positions, head_size)
    prepare_rows = partial(head_prepare, cosine_rows=cosine_rows, sine_rows=sine_rows)
    query_raw = matmul(normed_input, full_query).reshape(row_count, query_heads, head_size)
    unrotated_keys = matmul(normed_input, full_key).reshape(row_count, key_heads, head_size)
    values_local = matmul(normed_input, full_value).astype(jnp.bfloat16)
    gate_logits = matmul(normed_input, full_gate)
    query_rotated, query_pull = jax.vjp(prepare_rows, query_raw, query_gain)
    key_rotated, key_pull = jax.vjp(prepare_rows, unrotated_keys, key_gain)
    query_matrix = query_rotated.astype(jnp.bfloat16).reshape(
        row_count, key_heads, group_width, head_size
    )
    keys_local = key_rotated.astype(jnp.bfloat16).reshape(row_count, key_width)
    keys_all, values_all = (
        lax.all_gather(keys_local, "seq", axis=0, tiled=True),
        lax.all_gather(values_local, "seq", axis=0, tiled=True),
    )
    block_count = (seq_place * row_count + row_count + block_length - 1) // block_length

    def block_scores(key_rows, block_start):
        key_block = lax.dynamic_slice_in_dim(key_rows, block_start, block_length, 0).reshape(
            block_length, key_heads, head_size
        )
        raw_scores = jnp.einsum(
            "qgrd,kgd->grqk", query_matrix, key_block, preferred_element_type=jnp.float32
        )
        key_positions = block_start + jnp.arange(block_length, dtype=jnp.int32)
        allowed = key_positions[None, :] <= positions[:, None]
        return jnp.where(allowed, raw_scores * scale_factor, -1e30)

    def stats_step(block_index, stat_pair):
        running_max, running_sum = stat_pair
        scores = block_scores(keys_all, block_index * block_length)
        new_max = jnp.maximum(running_max, jnp.max(scores, axis=-1))
        running_sum = running_sum * jnp.exp(running_max - new_max) + jnp.sum(
            jnp.exp(scores - new_max[..., None]), axis=-1
        )
        return (new_max, running_sum)

    stat_shape = (key_heads, group_width, row_count)
    row_max, row_sum = lax.fori_loop(
        0,
        block_count,
        stats_step,
        (jnp.full(stat_shape, -1e30, jnp.float32), jnp.zeros(stat_shape, jnp.float32)),
    )

    def value_step(block_index, partial_out):
        block_start = block_index * block_length
        softmax_rows = (
            jnp.exp(block_scores(keys_all, block_start) - row_max[..., None]) / row_sum[..., None]
        ).astype(jnp.bfloat16)
        value_block = lax.dynamic_slice_in_dim(values_all, block_start, block_length, 0).reshape(
            block_length, key_heads, head_size
        )
        return partial_out + jnp.einsum(
            "grqk,kgd->qgrd", softmax_rows, value_block, preferred_element_type=jnp.float32
        )

    attended = lax.fori_loop(
        0,
        block_count,
        value_step,
        jnp.zeros((row_count, key_heads, group_width, head_size), jnp.float32),
    ).reshape(row_count, query_heads, head_size)
    gated_value, gate_pull = jax.vjp(apply_gate, attended, gate_logits)
    gated_rows = gated_value.astype(jnp.bfloat16).reshape(row_count, query_heads * head_size)
    attention_out = lax.psum(matmul(gated_rows, full_out).astype(jnp.bfloat16), "grp").astype(
        jnp.float32
    )
    hidden = input_rows + attention_out
    full_feed_gate, full_feed_up, full_feed_down = (
        lax.all_gather(feed_gate, "seq", axis=0, tiled=True),
        lax.all_gather(feed_up, "seq", axis=0, tiled=True),
        lax.all_gather(feed_down, "seq", axis=1, tiled=True),
    )
    normed_mlp_value, feed_norm_pull = jax.vjp(rms_norm, hidden, feed_gain)
    normed_mlp = normed_mlp_value.astype(jnp.bfloat16)
    gate_part = matmul(normed_mlp, full_feed_gate)
    up_part = matmul(normed_mlp, full_feed_up)
    mixed_value, swiglu_pull = jax.vjp(swiglu, gate_part, up_part)
    mixed_rows = mixed_value.astype(jnp.bfloat16)
    feed_out = lax.psum(matmul(mixed_rows, full_feed_down).astype(jnp.bfloat16), "grp").astype(
        jnp.float32
    )
    output = (hidden + feed_out).astype(jnp.bfloat16)
    grad_rows = cotangent.astype(jnp.float32)
    grad_feed_down = inner(mixed_rows, cotangent)
    grad_gate_part, grad_up_part = swiglu_pull(outer(cotangent, full_feed_down))
    grad_gate_low = grad_gate_part.astype(jnp.bfloat16)
    grad_up_low = grad_up_part.astype(jnp.bfloat16)
    grad_feed_gate = inner(normed_mlp, grad_gate_low)
    grad_feed_up = inner(normed_mlp, grad_up_low)
    grad_normed_mlp = lax.psum(
        (outer(grad_gate_low, full_feed_gate) + outer(grad_up_low, full_feed_up)).astype(
            jnp.bfloat16
        ),
        "grp",
    ).astype(jnp.float32)
    grad_hidden_norm, grad_feed_gain = feed_norm_pull(grad_normed_mlp)
    grad_hidden = grad_rows + grad_hidden_norm
    hidden_low = grad_hidden.astype(jnp.bfloat16)
    grad_out_weight = inner(gated_rows, hidden_low)
    grad_gated = outer(hidden_low, full_out).reshape(row_count, query_heads, head_size)
    grad_attended, grad_logits = gate_pull(grad_gated)
    grad_attended_low = grad_attended.astype(jnp.bfloat16).reshape(
        row_count, key_heads, group_width, head_size
    )
    grad_logits_low = grad_logits.astype(jnp.bfloat16)
    attended_grouped = attended.reshape(row_count, key_heads, group_width, head_size)
    row_delta = jnp.sum(
        grad_attended_low.astype(jnp.float32) * attended_grouped, axis=-1
    ).transpose(1, 2, 0)

    def block_grads(block_start):
        softmax_rows = (
            jnp.exp(block_scores(keys_all, block_start) - row_max[..., None]) / row_sum[..., None]
        )
        key_block = lax.dynamic_slice_in_dim(keys_all, block_start, block_length, 0).reshape(
            block_length, key_heads, head_size
        )
        value_block = lax.dynamic_slice_in_dim(values_all, block_start, block_length, 0).reshape(
            block_length, key_heads, head_size
        )
        grad_probs = jnp.einsum(
            "qgrd,kgd->grqk", grad_attended_low, value_block, preferred_element_type=jnp.float32
        )
        grad_scores = (softmax_rows * (grad_probs - row_delta[..., None]) * scale_factor).astype(
            jnp.bfloat16
        )
        query_term = jnp.einsum(
            "grqk,kgd->qgrd", grad_scores, key_block, preferred_element_type=jnp.float32
        )
        return (softmax_rows, grad_scores, query_term)

    query_zero = jnp.zeros((row_count, key_heads, group_width, head_size), jnp.float32)

    def back_step(block_index, back_carry):
        grad_queries, grad_keys, grad_values = back_carry
        block_start = block_index * block_length
        softmax_rows, grad_scores, query_term = block_grads(block_start)
        key_term = jnp.einsum(
            "grqk,qgrd->kgd", grad_scores, query_matrix, preferred_element_type=jnp.float32
        ).reshape(block_length, key_width)
        value_term = jnp.einsum(
            "grqk,qgrd->kgd",
            softmax_rows.astype(jnp.bfloat16),
            grad_attended_low,
            preferred_element_type=jnp.float32,
        ).reshape(block_length, key_width)
        grad_keys = lax.dynamic_update_slice_in_dim(grad_keys, key_term, block_start, 0)
        grad_values = lax.dynamic_update_slice_in_dim(grad_values, value_term, block_start, 0)
        return (grad_queries + query_term, grad_keys, grad_values)

    grad_queries, grad_keys, grad_values = lax.fori_loop(
        0,
        block_count,
        back_step,
        (
            query_zero,
            jnp.zeros((total_rows, key_width), jnp.float32),
            jnp.zeros((total_rows, key_width), jnp.float32),
        ),
    )
    grad_keys_own, grad_values_own = (
        lax.psum_scatter(grad_keys, "seq", scatter_dimension=0, tiled=True),
        lax.psum_scatter(grad_values, "seq", scatter_dimension=0, tiled=True),
    )
    grad_query_raw, grad_query_gain = query_pull(
        grad_queries.reshape(row_count, query_heads, head_size)
    )
    grad_key_raw, grad_key_gain = key_pull(grad_keys_own.reshape(row_count, key_heads, head_size))
    grad_query_low = grad_query_raw.astype(jnp.bfloat16).reshape(row_count, query_heads * head_size)
    grad_key_low = grad_key_raw.astype(jnp.bfloat16).reshape(row_count, key_width)
    grad_value_low = grad_values_own.astype(jnp.bfloat16)
    grad_query_weight = inner(normed_input, grad_query_low)
    grad_key_weight = inner(normed_input, grad_key_low)
    grad_value_weight = inner(normed_input, grad_value_low)
    grad_gate_weight = inner(normed_input, grad_logits_low)
    partial_normed = (
        outer(grad_query_low, full_query)
        + outer(grad_key_low, full_key)
        + outer(grad_value_low, full_value)
        + outer(grad_logits_low, full_gate)
    )
    grad_normed = lax.psum(partial_normed.astype(jnp.bfloat16), "grp").astype(jnp.float32)
    grad_input_norm, grad_attention_gain = attention_norm_pull(grad_normed)
    grad_inputs = (grad_hidden + grad_input_norm).astype(jnp.bfloat16)
    gain_totals = lax.psum((grad_query_gain, grad_key_gain), ("seq", "grp"))
    (
        sum_query,
        sum_key,
        sum_value,
        sum_gate,
        sum_out,
        sum_attention_gain,
        sum_feed_gate,
        sum_feed_up,
        sum_feed_down,
        sum_feed_gain,
    ) = (
        lax.psum_scatter(grad_query_weight, "seq", scatter_dimension=0, tiled=True),
        lax.psum_scatter(grad_key_weight, "seq", scatter_dimension=0, tiled=True),
        lax.psum_scatter(grad_value_weight, "seq", scatter_dimension=0, tiled=True),
        lax.psum_scatter(grad_gate_weight, "seq", scatter_dimension=0, tiled=True),
        lax.psum_scatter(grad_out_weight, "seq", scatter_dimension=1, tiled=True),
        lax.psum_scatter(grad_attention_gain, "seq", scatter_dimension=0, tiled=True),
        lax.psum_scatter(grad_feed_gate, "seq", scatter_dimension=0, tiled=True),
        lax.psum_scatter(grad_feed_up, "seq", scatter_dimension=0, tiled=True),
        lax.psum_scatter(grad_feed_down, "seq", scatter_dimension=1, tiled=True),
        lax.psum_scatter(grad_feed_gain, "seq", scatter_dimension=0, tiled=True),
    )
    return (
        output,
        grad_inputs,
        sum_attention_gain,
        sum_query,
        sum_key,
        sum_value,
        sum_gate,
        gain_totals[0],
        gain_totals[1],
        sum_out,
        sum_feed_gain,
        sum_feed_gate,
        sum_feed_up,
        sum_feed_down,
    )


def solution(mesh):
    in_specs = (
        P("seq", None),
        P(),
        P("seq", "grp"),
        P("seq", "grp"),
        P("seq", "grp"),
        P("seq", "grp"),
        P(),
        P(),
        P("grp", "seq"),
        P(),
        P("seq", "grp"),
        P("seq", "grp"),
        P("grp", "seq"),
        P("seq", None),
    )
    out_specs = (
        P("seq", None),
        P("seq", None),
        P("seq"),
        P("seq", "grp"),
        P("seq", "grp"),
        P("seq", "grp"),
        P("seq", "grp"),
        P(),
        P(),
        P("grp", "seq"),
        P("seq"),
        P("seq", "grp"),
        P("seq", "grp"),
        P("grp", "seq"),
    )
    return jax.shard_map(
        per_device, mesh=mesh, in_specs=in_specs, out_specs=out_specs, check_vma=False
    )
```

profile of v0, /device:TPU:1, one launch (start us, length us, event | category | flops | bytes accessed | tf_op | source)
XLA Modules:
  0.0 4370.8 jit_solution(2103647805394180239)
XLA Ops:
  10.7 105.9 %all-gather.11.cloned.1.call-done = bf16[2048,512]{1,0:T(8,128)(2,1)} async-done(((bf16[32,512]{1,0:T(8,128)(2,1)}), bf16[2048,512]{1,0:T(8,128)(2,1)}) %all-gather.11.cloned.1.call-update) | async-done | bytes 2097168 | tf_op jit(solution)/shard_map/all_gather | solution.py:92
  119.9 100.7 %all-gather.15.cloned.1.call-done = bf16[2048,512]{1,0:T(8,128)(2,1)} async-done(((bf16[32,512]{1,0:T(8,128)(2,1)}), bf16[2048,512]{1,0:T(8,128)(2,1)}) %all-gather.15.cloned.1.call-update) | async-done | bytes 2097168 | tf_op jit(solution)/shard_map/all_gather | solution.py:91
  225.4 79.7 %all-gather = bf16[64,32,8]{1,2,0:T(8,128)(2,1)S(1)} all-gather(bf16[1,32,8]{1,2,0:T(8,128)(2,1)S(1)} %bitcast.272), channel_id=1, replica_groups=mesh['seq'=64,'grp'=2] {'seq'}, dimensions={0}, use_global_device_ids=true | all-gather | bytes 33280 | tf_op jit(solution)/shard_map/all_gather | solution.py:93
  305.7 21.7 all-gather.19.cloned.1.call-done
  331.9 107.8 %all-gather.13.cloned.1.call-done = bf16[8192,512]{1,0:T(8,128)(2,1)} async-done(((bf16[128,512]{1,0:T(8,128)(2,1)}), bf16[8192,512]{1,0:T(8,128)(2,1)}) %all-gather.13.cloned.1.call-update) | async-done | bytes 8388624 | tf_op jit(solution)/shard_map/all_gather | solution.py:118
  439.7 12.0 copy.162
  451.7 117.7 %all-gather.17.cloned.1.call-done = bf16[8192,512]{0,1:T(8,128)(2,1)} async-done(((bf16[128,512]{0,1:T(8,128)(2,1)}), bf16[8192,512]{0,1:T(8,128)(2,1)}) %all-gather.17.cloned.1.call-update) | async-done | bytes 8388624 | tf_op jit(solution)/shard_map/all_gather | solution.py:117
  574.3 102.2 %all-gather.21.cloned.1.call-done = bf16[1024,2048]{0,1:T(8,128)(2,1)} async-done(((bf16[1024,32]{0,1:T(8,128)(2,1)}), bf16[1024,2048]{0,1:T(8,128)(2,1)}) %all-gather.21.cloned.1.call-update) | async-done | bytes 4194320 | tf_op jit(solution)/shard_map/all_gather | solution.py:94
  683.6 33.0 all-reduce.13.cloned.1.call-done
  719.2 116.9 %all-gather.25.cloned.1.call-done = bf16[2048,3072]{1,0:T(8,128)(2,1)} async-done(((bf16[32,3072]{1,0:T(8,128)(2,1)}), bf16[2048,3072]{1,0:T(8,128)(2,1)}) %all-gather.25.cloned.1.call-update) | async-done | bytes 12582928 | tf_op jit(solution)/shard_map/all_gather | solution.py:176
  843.7 111.7 %all-gather.23.cloned.1.call-done = bf16[2048,3072]{1,0:T(8,128)(2,1)} async-done(((bf16[32,3072]{1,0:T(8,128)(2,1)}), bf16[2048,3072]{1,0:T(8,128)(2,1)}) %all-gather.23.cloned.1.call-update) | async-done | bytes 12582928 | tf_op jit(solution)/shard_map/all_gather | solution.py:175
  962.9 111.6 %all-gather.27.cloned.1.call-done = bf16[3072,2048]{0,1:T(8,128)(2,1)} async-done(((bf16[3072,32]{0,1:T(8,128)(2,1)}), bf16[3072,2048]{0,1:T(8,128)(2,1)}) %all-gather.27.cloned.1.call-update) | async-done | bytes 12582928 | tf_op jit(solution)/shard_map/all_gather | solution.py:177
  1101.0 35.8 all-reduce.15.cloned.1.call-done
  1189.0 376.1 %reduce-scatter.13.cloned.1.call-done = f32[128,512]{0,1:T(8,128)} async-done(((f32[8192,512]{0,1:T(8,128)}), f32[128,512]{0,1:T(8,128)}) %reduce-scatter.13.cloned.1.call-update) | async-done | bytes 262160 | tf_op jit(solution)/shard_map/reduce_scatter | solution.py:268
  1571.5 303.9 %reduce-scatter.15.cloned.1.call-done = f32[128,512]{0,1:T(8,128)} async-done(((f32[8192,512]{0,1:T(8,128)}), f32[128,512]{0,1:T(8,128)}) %reduce-scatter.15.cloned.1.call-update) | async-done | bytes 262160 | tf_op jit(solution)/shard_map/reduce_scatter | solution.py:269
  1931.8 228.3 %reduce-scatter.31.cloned.1.call-done = f32[32,8]{1,0:T(8,128)} async-done(((f32[2048,8]{1,0:T(8,128)}), f32[32,8]{1,0:T(8,128)}) %reduce-scatter.31.cloned.1.call-update) | async-done | bytes 1040
  2161.5 81.5 %all-reduce.6 = (f32[128]{0:T(128)}, f32[128]{0:T(128)}) all-reduce(f32[128]{0:T(128)S(1)} %copy-done.35, f32[128]{0:T(128)S(1)} %get-tuple-element.414), channel_id=1, replica_groups=mesh['seq'=64,'grp'=2] {'seq','grp'}, use_global_device_ids=true, to_apply=%region_31.32 | all-reduce | flops 256 | bytes 2048 | tf_op jit(solution)/shard_map/psum | solution.py:291
  2244.6 269.6 %all-reduce.7 = (f32[2048]{0:T(1024)S(1)}, f32[2048]{0:T(1024)S(1)}) all-reduce(f32[2048]{0:T(1024)S(1)} %get-tuple-element.412, f32[2048]{0:T(1024)S(1)} %get-tuple-element.408), channel_id=4, replica_groups=mesh['seq'=64,'grp'=2] {'seq'}, use_global_device_ids=true, to_apply=%region_25.26.clone | all-reduce | flops 4096 | bytes 32768
  2518.4 288.3 %reduce-scatter.17.cloned.1.call-done = f32[32,1024]{1,0:T(8,128)} async-done(((f32[2048,1024]{1,0:T(8,128)}), f32[32,1024]{1,0:T(8,128)}) %reduce-scatter.17.cloned.1.call-update) | async-done | bytes 131088 | tf_op jit(solution)/shard_map/reduce_scatter | solution.py:304
  2806.7 288.6 %reduce-scatter.21.cloned.1.call-done = f32[32,512]{1,0:T(8,128)} async-done(((f32[2048,512]{1,0:T(8,128)}), f32[32,512]{1,0:T(8,128)}) %reduce-scatter.21.cloned.1.call-update) | async-done | bytes 65552 | tf_op jit(solution)/shard_map/reduce_scatter | solution.py:306
  3095.4 289.7 %reduce-scatter.19.cloned.1.call-done = f32[32,512]{1,0:T(8,128)} async-done(((f32[2048,512]{1,0:T(8,128)}), f32[32,512]{1,0:T(8,128)}) %reduce-scatter.19.cloned.1.call-update) | async-done | bytes 65552 | tf_op jit(solution)/shard_map/reduce_scatter | solution.py:305
  3385.1 326.7 %reduce-scatter.29.cloned.1.call-done = f32[3072,32]{0,1:T(8,128)} async-done(((f32[3072,2048]{0,1:T(8,128)}), f32[3072,32]{0,1:T(8,128)}) %reduce-scatter.29.cloned.1.call-update) | async-done | bytes 393232 | tf_op jit(solution)/shard_map/reduce_scatter | solution.py:312
  3711.7 326.3 %reduce-scatter.27.cloned.1.call-done = f32[32,3072]{1,0:T(8,128)} async-done(((f32[2048,3072]{1,0:T(8,128)}), f32[32,3072]{1,0:T(8,128)}) %reduce-scatter.27.cloned.1.call-update) | async-done | bytes 393232 | tf_op jit(solution)/shard_map/reduce_scatter | solution.py:311
  4038.0 325.5 %reduce-scatter.25.cloned.1.call-done = f32[32,3072]{1,0:T(8,128)} async-done(((f32[2048,3072]{1,0:T(8,128)}), f32[32,3072]{1,0:T(8,128)}) %reduce-scatter.25.cloned.1.call-update) | async-done | bytes 393232 | tf_op jit(solution)/shard_map/reduce_scatter | solution.py:310
  (245 shorter events, 204.5 us)
Async XLA Ops:
  7.2 109.4 %all-gather.11.cloned.1.call-start = ((), (), s32[]{:S(2)}) async-start(), calls=%async_computation.10 | async-start | bytes 2129920 | tf_op jit(solution)/shard_map/all_gather | solution.py:92
  7.9 212.7 %all-gather.15.cloned.1.call-start = ((), (), s32[]{:S(2)}) async-start(), calls=%async_computation.12 | async-start | bytes 2129920 | tf_op jit(solution)/shard_map/all_gather | solution.py:91
  8.7 318.7 %all-gather.19.cloned.1.call-start = ((), (), s32[]{:S(2)}) async-start(), calls=%async_computation.14 | async-start | bytes 4259840 | tf_op jit(solution)/shard_map/all_gather | solution.py:90
  9.4 430.3 %all-gather.13.cloned.1.call-start = ((), (), s32[]{:S(2)}) async-start(), calls=%async_computation.11 | async-start | bytes 8519680 | tf_op jit(solution)/shard_map/all_gather | solution.py:118
  119.5 449.8 %all-gather.17.cloned.1.call-start = ((), (), s32[]{:S(2)}) async-start(), calls=%async_computation.13 | async-start | bytes 8519680 | tf_op jit(solution)/shard_map/all_gather | solution.py:117
  224.8 451.7 %all-gather.21.cloned.1.call-start = ((), (), s32[]{:S(2)}) async-start(), calls=%async_computation.15 | async-start | bytes 4259840 | tf_op jit(solution)/shard_map/all_gather | solution.py:94
  225.4 491.2 %all-reduce.13.cloned.1.call-start = ((), (), s32[]{:S(2)}) async-start(), calls=%async_computation.16 | async-start | bytes 1048576 | tf_op jit(solution)/shard_map/psum | solution.py:170
  681.0 155.1 %all-gather.25.cloned.1.call-start = ((), (), s32[]{:S(2)}) async-start(), calls=%async_computation.18 | async-start | bytes 12779520 | tf_op jit(solution)/shard_map/all_gather | solution.py:176
  681.8 273.6 %all-gather.23.cloned.1.call-start = ((), (), s32[]{:S(2)}) async-start(), calls=%async_computation.17 | async-start | bytes 12779520 | tf_op jit(solution)/shard_map/all_gather | solution.py:175
  682.5 391.9 %all-gather.27.cloned.1.call-start = ((), (), s32[]{:S(2)}) async-start(), calls=%async_computation.19 | async-start | bytes 12779520 | tf_op jit(solution)/shard_map/all_gather | solution.py:177
  683.1 453.6 %all-reduce.15.cloned.1.call-start = ((), (), s32[]{:S(2)}) async-start(), calls=%async_computation.20 | async-start | bytes 1048576 | tf_op jit(solution)/shard_map/psum | solution.py:196
  1100.9 464.2 %reduce-scatter.13.cloned.1.call-start = ((), (), s32[]{:S(2)}) async-start(), calls=%async_computation.21 | async-start | bytes 17039360 | tf_op jit(solution)/shard_map/reduce_scatter | solution.py:268
  1165.0 710.4 %reduce-scatter.15.cloned.1.call-start = ((), (), s32[]{:S(2)}) async-start(), calls=%async_computation.22 | async-start | bytes 17039360 | tf_op jit(solution)/shard_map/reduce_scatter | solution.py:269
  1165.8 994.3 %reduce-scatter.31.cloned.1.call-start = ((), (), s32[]{:S(2)}) async-start(), calls=%async_computation.30 | async-start | bytes 1064960
  1184.3 1058.7 %all-reduce.17.cloned.1.call-start = ((), (), s32[]{:S(2)}) async-start(), calls=%async_computation.31 | async-start | bytes 2097152 | tf_op jit(solution)/shard_map/psum | solution.py:185
  1189.0 377.6 %copy-start.25 = (f32[128]{0:T(128)S(1)}, f32[128]{0:T(128)}, u32[]{:S(2)}) copy-start(f32[128]{0:T(128)} %param.27) | copy-start | bytes 1540
  1879.4 639.0 %reduce-scatter.23.cloned.1.call-start = ((), (), s32[]{:S(2)}) async-start(), calls=%async_computation.26 | async-start | bytes 8519680 | tf_op jit(solution)/shard_map/reduce_scatter | solution.py:308
  1884.2 922.5 %reduce-scatter.17.cloned.1.call-start = ((), (), s32[]{:S(2)}) async-start(), calls=%async_computation.23 | async-start | bytes 8519680 | tf_op jit(solution)/shard_map/reduce_scatter | solution.py:304
  1889.0 1206.4 %reduce-scatter.21.cloned.1.call-start = ((), (), s32[]{:S(2)}) async-start(), calls=%async_computation.25 | async-start | bytes 4259840 | tf_op jit(solution)/shard_map/reduce_scatter | solution.py:306
  1892.7 1492.4 %reduce-scatter.19.cloned.1.call-start = ((), (), s32[]{:S(2)}) async-start(), calls=%async_computation.24 | async-start | bytes 4259840 | tf_op jit(solution)/shard_map/reduce_scatter | solution.py:305
  1895.9 1815.9 %reduce-scatter.29.cloned.1.call-start = ((), (), s32[]{:S(2)}) async-start(), calls=%async_computation.29 | async-start | bytes 25559040 | tf_op jit(solution)/shard_map/reduce_scatter | solution.py:312
  1907.2 2130.8 %reduce-scatter.27.cloned.1.call-start = ((), (), s32[]{:S(2)}) async-start(), calls=%async_computation.28 | async-start | bytes 25559040 | tf_op jit(solution)/shard_map/reduce_scatter | solution.py:311
  1918.6 2445.0 %reduce-scatter.25.cloned.1.call-start = ((), (), s32[]{:S(2)}) async-start(), calls=%async_computation.27 | async-start | bytes 25559040 | tf_op jit(solution)/shard_map/reduce_scatter | solution.py:310
  1929.9 585.4 %copy-start.32 = (f32[128]{0:T(128)S(1)}, f32[128]{0:T(128)}, u32[]{:S(2)}) copy-start(f32[128]{0:T(128)} %copy-done.31) | copy-start | bytes 1540
  (38 other events, 3243.1 us)
Sparse Core Ops, SparseCore 0:
  9.8 106.7 all-gather.10
  118.3 102.3 all-gather.14
  222.4 104.9 all-gather.18
  329.5 110.1 all-gather.12
  441.7 127.6 all-gather.16
  571.0 105.4 all-gather.20
  681.1 35.3 all-reduce.12
  718.4 117.6 all-gather.24
  837.9 117.3 all-gather.22
  957.0 117.3 all-gather.26
  1101.1 35.6 all-reduce.14
  1165.1 399.9 reduce-scatter.12
  1567.5 307.8 reduce-scatter.14
  1877.6 282.4 reduce-scatter.30
  2163.2 50.8 all-reduce.16
  2216.8 292.1 reduce-scatter.22
  2511.8 294.8 reduce-scatter.16
  2809.5 285.8 reduce-scatter.20
  3098.4 286.5 reduce-scatter.18
  3387.9 323.7 reduce-scatter.28
  3714.7 323.2 reduce-scatter.26
  4041.0 322.4 reduce-scatter.24
where the time goes:
time: 4390 us; the launch traced here: 4370 us
  waiting for transfers between devices  3720 us (85%)
  blocking collectives  431 us (10%)
  matrix products  135 us (3%)
  local copies, waits for them, and re-layouts  45 us (1%)
    reduce_scatter x1, waiting for transfers between devices, per_device(): lax.psum_scatter(grad_keys, 'seq', scatter_dimension=0, tiled=True)  376 us
    reduce_scatter x1, waiting for transfers between devices, per_device(): lax.psum_scatter(grad_feed_down, 'seq', scatter_dimension=1, tiled=True)  327 us
    reduce_scatter x1, waiting for transfers between devices, per_device(): lax.psum_scatter(grad_feed_up, 'seq', scatter_dimension=0, tiled=True)  326 us
    reduce_scatter x1, waiting for transfers between devices, per_device(): lax.psum_scatter(grad_feed_gate, 'seq', scatter_dimension=0, tiled=True)  326 us
    reduce_scatter x1, waiting for transfers between devices, per_device(): lax.psum_scatter(grad_values, 'seq', scatter_dimension=0, tiled=True)  304 us
    reduce_scatter x1, waiting for transfers between devices, per_device(): lax.psum_scatter(grad_key_weight, 'seq', scatter_dimension=0, tiled=True)  290 us
    reduce_scatter x1, waiting for transfers between devices, per_device(): lax.psum_scatter(grad_value_weight, 'seq', scatter_dimension=0, tiled=True)  289 us
    reduce_scatter x1, waiting for transfers between devices, per_device(): lax.psum_scatter(grad_query_weight, 'seq', scatter_dimension=0, tiled=True)  288 us
  transfers between devices with their start and end apart: 22, of which 20 were waited for; matrix products, arithmetic and copies ran while one was open for 3% of the time, Pallas kernels for 0%

commit v1 on v0

v1 whole, which is shorter than its diff:
```python
from types import SimpleNamespace

import jax
import jax.numpy as jnp
from jax import lax
from jax.experimental import pallas as pl
from jax.experimental.pallas import tpu as pltpu
from jax.sharding import PartitionSpec as P

EPSILON = 1e-06
ROPE_BASE = 1000000.0
WIDTH = 2048
HEAD = 128
EIGHTH = 768
ATT = 896
PROJ = 640
SCALE = HEAD**-0.5
LOG2E = 1.4426950408889634
LN2 = 0.6931471805599453
BF, F32 = jnp.bfloat16, jnp.float32
MESH = pl.DeviceIdType.MESH
ALL = slice(None)


def mm(a, b):
    return jnp.dot(a, b, preferred_element_type=F32)


def mm_tb(a, b):
    return lax.dot_general(a, b, (((1,), (1,)), ((), ())), preferred_element_type=F32)


def rms_scale(v):
    return lax.rsqrt(jnp.mean(v * v, axis=-1, keepdims=True) + EPSILON)


def rms_back(v, gain, dy):
    r = rms_scale(v)
    u = gain * dy
    dv = r * (u - v * (r * r * jnp.mean(u * v, axis=-1, keepdims=True)))
    return dv, jnp.sum(dy * v * r, axis=0, keepdims=True)


def rope(v, cos, sin):
    return v * cos + pltpu.roll(v, HEAD // 2, 1) * sin


def rope_back(v, cos, sin):
    return v * cos + pltpu.roll(v * sin, HEAD // 2, 1)


def three_parts(v, lanes):
    hi = v.astype(BF).astype(F32)
    mid = (v - hi).astype(BF).astype(F32)
    low = v - hi - mid
    return jnp.where(
        lanes == 0, hi, jnp.where(lanes == 1, mid, jnp.where(lanes == 2, low, 0.0))
    ).astype(BF)


def select(row_of, shape):
    row = lax.broadcasted_iota(jnp.int32, shape, 0)
    col = lax.broadcasted_iota(jnp.int32, shape, 1)
    return jnp.where(row_of(row, col), 1.0, 0.0).astype(BF)


def body(R):
    s, zh = lax.axis_index("seq"), lax.axis_index("grp")
    c = lax.rem(s, 2)
    x = lax.rem(lax.div(s, 2), 4)
    y = lax.rem(lax.div(s, 8), 4)
    zl = lax.div(s, 32)
    z = zh * 2 + zl
    j = y * 4 + x
    me = zl * 2 + c

    def up(v, k):
        return lax.rem(v + k, 4)

    def dev(zz, yy, xx, cc):
        return (lax.rem(zz, 2) * 32 + yy * 8 + xx * 2 + cc, lax.div(zz, 2))

    sib = dev(z, y, x, 1 - c)
    zs = [up(z, 1), up(z, 3), up(z, 2)]
    zdev = [dev(v, y, x, c) for v in zs]
    part = (zl_dev := (1 - zl) * 32 + y * 8 + x * 2 + c, zh)
    diag = ((1 - zl) * 32 + y * 8 + x * 2 + 1 - c, zh)
    other = (zl_dev, 1 - zh)
    xdev = [dev(z, y, up(x, k), c) for k in (1, 3, 2)]
    ydev = [dev(z, up(y, k), x, c) for k in (1, 3, 2)]

    barrier = pltpu.get_barrier_semaphore()
    greet = [sib, diag] + zdev + xdev + ydev
    for d in greet:
        pl.semaphore_signal(barrier, inc=1, device_id=d, device_id_type=MESH)

    count = [0]

    def ids(k):
        count[0] += k
        return count[0] - k

    class Group:
        def __init__(self, k):
            self.base, self.sent = ids(k), []

        def copy(self, src, dst, d, i):
            i += self.base
            return pltpu.make_async_remote_copy(
                src_ref=src, dst_ref=dst, send_sem=R.send.at[i], recv_sem=R.recv.at[i],
                device_id=d, device_id_type=MESH,
            )

        def go(self, src, dst, d, i):
            cp = self.copy(src, dst, d, i)
            cp.start()
            self.sent.append(cp)

        def got(self, ref, i):
            self.copy(ref, ref, sib, i).wait_recv()

        def end(self):
            for cp in self.sent:
                cp.wait_send()

    def exchange(buf, wl):
        g = Group(3)

        def start():
            buf[zl, y, x, c] = wl[me]
            dst = buf.at[zl, y, x, c]
            g.go(wl.at[zl * 2 + 1 - c], dst, sib, 0)
            g.go(wl.at[(1 - zl) * 2 + c], dst, part, 1)
            g.go(wl.at[(1 - zl) * 2 + 1 - c], dst, diag, 2)

        def wait():
            g.got(buf.at[zl, y, x, 1 - c], 0)
            g.got(buf.at[1 - zl, y, x, c], 1)
            g.got(buf.at[1 - zl, y, x, 1 - c], 2)

        return start, wait, g.end

    def give_back(src, dst):
        g = Group(3)

        def start():
            dst[me] = src[zl, y, x, c]
            g.go(src.at[zl, y, x, 1 - c], dst.at[me], sib, 0)
            g.go(src.at[1 - zl, y, x, c], dst.at[me], part, 1)
            g.go(src.at[1 - zl, y, x, 1 - c], dst.at[me], diag, 2)

        def wait():
            g.got(dst.at[zl * 2 + 1 - c], 0)
            g.got(dst.at[(1 - zl) * 2 + c], 1)
            g.got(dst.at[(1 - zl) * 2 + 1 - c], 2)

        return start, wait, g.end

    a_y = SimpleNamespace(
        full=lambda p: (0, p), half=lambda p, h: (0, p, ALL, h), elem=lambda p, k, h: (0, p, k, h),
        k=4, pos=y, dev=ydev,
    )
    a_x = SimpleNamespace(
        full=lambda p: (0, y, p), half=lambda p, h: (0, y, p, h), elem=lambda p, k, h: (0, y, p, h),
        k=1, pos=x, dev=xdev,
    )
    b_x = SimpleNamespace(
        full=lambda p: (1, ALL, p), half=lambda p, h: (1, ALL, p, h), elem=lambda p, k, h: (1, k, p, h),
        k=4, pos=x, dev=xdev,
    )
    b_y = SimpleNamespace(
        full=lambda p: (1, p, x), half=lambda p, h: (1, p, x, h), elem=lambda p, k, h: (1, p, x, h),
        k=1, pos=y, dev=ydev,
    )

    def gather_ring(buf, a):
        g, p = Group(4), a.pos

        def s1():
            mine = buf.at[a.full(p)]
            g.go(mine, mine, a.dev[0], 0)
            g.go(mine, mine, a.dev[1], 1)

        def s2():
            g.got(buf.at[a.full(up(p, 3))], 0)
            low = buf.at[a.half(up(p, 3), 0)]
            g.go(low, low, a.dev[0], 2)
            g.got(buf.at[a.full(up(p, 1))], 1)
            high = buf.at[a.half(up(p, 1), 1)]
            g.go(high, high, a.dev[1], 3)

        def s3():
            g.got(buf.at[a.half(up(p, 2), 0)], 2)
            g.got(buf.at[a.half(up(p, 2), 1)], 3)

        return s1, s2, s3, g.end

    def gather(buf):
        one = [gather_ring(buf, a_x), gather_ring(buf, b_y)]
        two = [gather_ring(buf, a_y), gather_ring(buf, b_x)]

        def t1():
            for r in one:
                r[0]()

        def t2():
            for r in one:
                r[1]()

        def t3():
            for r, q in zip(one, two):
                r[2]()
                q[0]()

        def t4():
            for r in two:
                r[1]()

        def t5():
            for r in two:
                r[2]()
            for r in one + two:
                r[3]()

        return t1, t2, t3, t4, t5

    def reduce_ring(buf, a, r2, r1, cs):
        g, p, k = Group(4), a.pos, a.k

        def slot(ref, i):
            if k == 1:
                return ref.at[(i, 0) + (ALL,) * (len(ref.shape) - 3) + (cs,)]
            return ref.at[(i,) + (ALL,) * (len(ref.shape) - 2) + (cs,)]

        def loop(fn):
            if k == 1:
                fn(0)
            else:
                pl.loop(0, k)(fn)

        def s1():
            g.go(buf.at[a.half(up(p, 2), 0)], slot(r2, 0), a.dev[0], 0)
            g.go(buf.at[a.half(up(p, 2), 1)], slot(r2, 1), a.dev[1], 1)

        def s2():
            for i, step in ((0, 1), (1, 3)):
                g.got(slot(r2, i), i)
                to = up(p, step)

                def add(q, i=i, to=to):
                    at = a.elem(to, q, i)
                    buf[at] = buf[at] + r2[i, q, :, cs]

                loop(add)
                g.go(buf.at[a.full(to)], slot(r1, i), a.dev[i], 2 + i)

        def s3():
            g.got(slot(r1, 0), 2)
            g.got(slot(r1, 1), 3)

            def add(q):
                for h in (0, 1):
                    at = a.elem(p, q, h)
                    total = (
                        buf[at].astype(F32)
                        + r1[0, q, h, :, cs].astype(F32)
                        + r1[1, q, h, :, cs].astype(F32)
                    )
                    buf[at] = total.astype(BF)

            loop(add)

        return s1, s2, s3, g.end

    def scatter(buf, bufs, cs):
        one = [
            reduce_ring(buf, a_y, bufs[0].at[0], bufs[1].at[0], cs),
            reduce_ring(buf, b_x, bufs[0].at[1], bufs[1].at[1], cs),
        ]
        two = [
            reduce_ring(buf, a_x, bufs[2].at[0], bufs[3].at[0], cs),
            reduce_ring(buf, b_y, bufs[2].at[1], bufs[3].at[1], cs),
        ]

        def t1():
            for r in one:
                r[0]()

        def t2():
            for r in one:
                r[1]()

        def t3():
            for r, q in zip(one, two):
                r[2]()
                q[0]()

        def t4():
            for r in two:
                r[1]()

        def t5():
            for r in two:
                r[2]()
            for r in one + two:
                r[3]()

        return t1, t2, t3, t4, t5

    def reduce_rows(pb, rsib, rz):
        g = Group(5)

        def s0():
            for t in (0, 1):
                g.go(pb.at[t * 2 + 1 - c], rsib.at[t], sib, t)

        def s1():
            for t in (0, 1):
                g.got(rsib.at[t], t)

                def add(h, t=t):
                    pb[t * 2 + c, h] = pb[t * 2 + c, h] + rsib[t, h]

                pl.loop(0, 2)(add)
            for i in range(3):
                zz = zs[i]
                src = pb.at[lax.rem(zz, 2) * 2 + c, lax.div(zz, 2)]
                g.go(src, rz.at[i], zdev[i], 2 + i)

        def s2():
            for i in range(3):
                g.got(rz.at[i], 2 + i)

        def total(rows):
            v = pb[me, zh, rows].astype(F32)
            for i in range(3):
                v = v + rz[i, rows].astype(F32)
            return v

        return s0, s1, s2, g.end, total

    def gather_rows(buf):
        g = Group(7)

        def place(zz, cc):
            return buf.at[lax.rem(zz, 2) * 2 + cc, lax.div(zz, 2)]

        def s0():
            mine = buf.at[me, zh]
            for i in range(3):
                g.go(mine, mine, zdev[i], i)
            g.go(mine, mine, sib, 3)

        came = [zs[1], zs[0], zs[2]]

        def s1():
            for i in range(3):
                at = place(came[i], c)
                g.got(at, i)
                g.go(at, at, sib, 4 + i)

        def s2():
            g.got(place(z, 1 - c), 3)
            for i in range(3):
                g.got(place(came[i], 1 - c), 4 + i)

        return s0, s1, s2, g.end

    def gather_blocks(buf):
        g = Group(5)

        def s0():
            g.go(buf.at[me, 0], buf.at[me, 0], part, 0)
            g.go(buf.at[me, 1], buf.at[me, 1], other, 1)
            g.go(buf.at[me], buf.at[me], sib, 2)

        def s1():
            for h in (0, 1):
                at = buf.at[(1 - zl) * 2 + c, h]
                g.got(at, h)
                g.go(at, at, sib, 3 + h)

        def s2():
            g.got(buf.at[zl * 2 + 1 - c], 2)
            for h in (0, 1):
                g.got(buf.at[(1 - zl) * 2 + 1 - c, h], 3 + h)

        return s0, s1, s2, g.end

    def twin(buf):
        g = Group(1)

        def start():
            g.go(buf.at[zh], buf.at[zh], zdev[2], 0)

        def wait():
            g.got(buf.at[1 - zh], 0)
            g.end()

        return start, wait

    for i in range(4):
        R.wla[i, :, 0:256] = R.qw[:, i * 256 : (i + 1) * 256]
        R.wla[i, :, 256:384] = R.kw[:, i * 128 : (i + 1) * 128]
        R.wla[i, :, 384:512] = R.vw[:, i * 128 : (i + 1) * 128]
        pick = select(lambda r, q, i=i: (r == q + 2 * i) & (q < 2), (8, 128))
        R.wla[i, :, 512:640] = mm(R.gw[...], pick).astype(BF)
        R.wla[i, :, 640:896] = R.ow[:, i * 256 : (i + 1) * 256]
    ex_a = exchange(R.wa, R.wla)
    ag_a = gather(R.wa)
    ex_m = exchange(R.wm, R.wlm)
    ag_m = gather(R.wm)
    ag_x = gather_blocks(R.xn)
    ag_c = gather_blocks(R.cot)
    ag_kv = gather(R.kv)

    pl.semaphore_wait(barrier, len(greet))
    ex_a[0]()

    @pl.loop(0, 4)
    def _(t):
        rows = pl.ds(pl.multiple_of(lax.rem(t, 2) * 32, 32), 32)
        v = R.x[pl.ds(pl.multiple_of(t * 32, 32), 32), :].astype(F32)
        R.xn[me, lax.div(t, 2), rows] = (v * rms_scale(v) * R.ag[...]).astype(BF)

    ag_x[0]()
    for i in range(4):
        R.wlm[i, :, 0:768] = R.fg[:, i * 768 : (i + 1) * 768]
        R.wlm[i, :, 768:1536] = R.fu[:, i * 768 : (i + 1) * 768]
        R.wlm[i, :, 1536:2304] = R.fd[:, i * 768 : (i + 1) * 768]
    R.cot[me] = R.ct[...].reshape(2, 64, WIDTH)
    ex_a[1]()
    ag_a[0]()
    ag_x[1]()
    ag_a[1]()
    ex_m[0]()
    ag_c[0]()
    ag_a[2]()
    ag_x[2]()
    ag_a[3]()
    ag_c[1]()
    ex_m[1]()
    ag_a[4]()
    ag_m[0]()

    @pl.loop(0, 4)
    def _(i):
        zi, ci = lax.div(i, 2), lax.rem(i, 2)
        w = R.wa[:, :, :, :, :, 0:PROJ].reshape(WIDTH, PROJ)
        raw = mm(R.xn[i].reshape(128, WIDTH), w)
        cos, sin = R.cos[i], R.sin[i]
        R.qraw[i] = raw[:, 0:256]
        R.kraw[i] = raw[:, 256:384]
        R.gl[i] = raw[:, 512:640]
        for h in (0, 1):
            v = raw[:, h * 128 : (h + 1) * 128]
            q = rope(v * rms_scale(v) * R.qg[...], cos, sin) * (SCALE * LOG2E)
            R.qx[zi, h, ci, :, 0:128] = q.astype(BF)
        v = raw[:, 256:384]
        k = rope(v * rms_scale(v) * R.kg[...], cos, sin)
        R.kv[zi, y, x, ci, :, 0:128] = k.astype(BF)
        R.kv[zi, y, x, ci, :, 128:256] = raw[:, 384:512].astype(BF)

    ag_kv[0]()
    ag_m[1]()
    ag_kv[1]()
    ag_kv[2]()
    ag_kv[3]()
    ag_kv[4]()
    ag_m[2]()

    ones = jnp.ones((256, 128), BF)
    key_i = lax.broadcasted_iota(jnp.int32, (512, 256), 1)
    row_i = lax.broadcasted_iota(jnp.int32, (512, 256), 0)
    seen = key_i <= lax.rem(row_i, 256)

    def tile(t):
        return (lax.div(t, 16), lax.rem(lax.div(t, 4), 4), lax.rem(t, 4))

    R.oacc[...] = jnp.zeros((2, 512, 256), F32)

    def forward(t, groups, diagonal):
        at = tile(t)
        k = R.kv[at + (ALL, ALL, slice(0, 128))].reshape(256, 128)
        v = R.kv[at + (ALL, ALL, slice(128, 256))].reshape(256, 128)
        v = jnp.concatenate([v, ones], axis=1)
        for g in groups:
            p = jnp.exp2(mm_tb(R.qx[g, :, :, :, 0:128].reshape(512, 128), k))
            if g == diagonal:
                p = jnp.where(seen, p, 0.0)
            R.oacc[g] += mm(p.astype(BF), v)

    @pl.loop(0, j)
    def _(t):
        forward(t, (0, 1), None)

    forward(j, (0, 1), 0)

    @pl.loop(j + 1, j + 16)
    def _(t):
        forward(t, (1,), None)

    forward(j + 16, (1,), 1)
    ag_m[3]()

    lanes = lax.broadcasted_iota(jnp.int32, (128, 128), 1)

    @pl.loop(0, 4)
    def _(i):
        zi, ci = lax.div(i, 2), lax.rem(i, 2)
        for h in (0, 1):
            rows = pl.ds(pl.multiple_of(h * 256 + ci * 128, 128), 128)
            total = R.oacc[zi, rows, 128:256]
            a = R.oacc[zi, rows, 0:128] / total
            R.att[i, :, h * 128 : (h + 1) * 128] = a
            R.qx[zi, h, ci, :, 128:256] = three_parts(-jnp.log2(total), lanes)
            gate = jax.nn.sigmoid(R.gl[i][:, h : h + 1])
            R.gated[i, :, h * 128 : (h + 1) * 128] = (a * gate).astype(BF)

    def spread(n, value):
        cols = pl.ds(pl.multiple_of(n * 256, 256), 256)
        return cols, value.reshape(4, 2, 64, 256).astype(BF)

    @pl.loop(0, 8)
    def _(n):
        w = R.wa[lax.div(n, 4), lax.rem(n, 4), :, :, :, PROJ:ATT].reshape(256, 256)
        cols, v = spread(n, mm_tb(R.gated[...].reshape(512, 256), w))
        R.pb[:, :, :, cols] = v

    rs1 = reduce_rows(R.pb, R.rsib, R.rz)
    ag_n = gather_rows(R.nm)
    rs1[0]()
    rs1[1]()
    rs1[2]()

    def owned(t):
        return pl.ds(pl.multiple_of(t * 16, 16), 16)

    @pl.loop(0, 4)
    def _(t):
        rows = owned(t)
        v = R.x[pl.ds(pl.multiple_of(zh * 64 + t * 16, 16), 16), :].astype(F32)
        v = v + rs1[4](rows)
        R.hid[rows] = v
        R.nm[me, zh, rows] = (v * rms_scale(v) * R.fgain[...]).astype(BF)

    rs1[3]()
    ex_a[2]()
    ex_m[2]()
    ag_n[0]()
    ag_c[2]()
    ag_m[4]()
    ag_n[1]()
    ag_n[2]()

    @pl.loop(0, 3)
    def _(n):
        cols = pl.ds(pl.multiple_of(n * 256, 256), 256)

        def weight(k):
            at = pl.ds(pl.multiple_of(k * 768 + n * 256, 256), 256)
            return R.wm[:, :, :, :, :, at].reshape(WIDTH, 256)

        rows = R.nm[...].reshape(512, WIDTH)
        gate = mm(rows, weight(0))
        upper = mm(rows, weight(1))
        grad = mm(R.cot[...].reshape(512, WIDTH), weight(2))
        sg = jax.nn.sigmoid(gate)
        silu = gate * sg
        R.act[0, :, cols] = (grad * upper * (sg * (1.0 + gate * (1.0 - sg)))).astype(BF)
        R.act[1, :, cols] = (grad * silu).astype(BF)
        R.act[2, :, cols] = (silu * upper).astype(BF)

    @pl.loop(0, 8)
    def _(n):
        at = (lax.div(n, 4), lax.rem(n, 4), ALL, ALL, ALL)
        v = mm_tb(R.act[0], R.wm[at + (slice(0, 768),)].reshape(256, 768))
        v = v + mm_tb(R.act[1], R.wm[at + (slice(768, 1536),)].reshape(256, 768))
        cols, v = spread(n, v)
        R.pb[:, :, :, cols] = v

    rs2 = reduce_rows(R.pb, R.rsib, R.rz)
    rs_f = reduce_rows(R.pb2, R.rsib2, R.rz2)
    rs2[0]()

    @pl.loop(0, 8)
    def _(n):
        at = (lax.div(n, 4), lax.rem(n, 4), ALL, ALL, ALL)
        w = R.wm[at + (slice(1536, 2304),)].reshape(256, 768)
        cols, v = spread(n, mm_tb(R.act[2], w))
        R.pb2[:, :, :, cols] = v

    rs2[1]()
    rs_f[0]()

    @pl.loop(0, 8)
    def _(n):
        at = (lax.div(n, 4), lax.rem(n, 4), ALL, ALL, ALL)
        cols = pl.ds(pl.multiple_of(n * 256, 256), 256)
        t = R.nm[:, :, :, cols].reshape(512, 256).T
        R.wm[at + (slice(0, 768),)] = mm(t, R.act[0]).astype(BF).reshape(4, 2, 32, 768)
        R.wm[at + (slice(768, 1536),)] = mm(t, R.act[1]).astype(BF).reshape(4, 2, 32, 768)
        t = R.cot[:, :, :, cols].reshape(512, 256).T
        R.wm[at + (slice(1536, 2304),)] = mm(t, R.act[2]).astype(BF).reshape(4, 2, 32, 768)

    ag_n[3]()
    for d in [sib] + zdev:
        pl.semaphore_signal(R.free, inc=1, device_id=d, device_id_type=MESH)

    big = (R.m_r2, R.m_r1, R.m_q2, R.m_q1)
    rs_m = scatter(R.wm, big, slice(0, 2304))
    ag_h = gather_rows(R.nm)
    rs_m[0]()
    rs_f[1]()
    rs2[2]()
    R.dgs[...] = jnp.zeros((2, WIDTH), F32)
    ag_c[3]()
    pl.semaphore_wait(R.free, 4)

    @pl.loop(0, 4)
    def _(t):
        rows = owned(t)
        dv, dg = rms_back(R.hid[rows], R.fgain[...], rs2[4](rows))
        dh = dv + R.ct[pl.ds(pl.multiple_of(zh * 64 + t * 16, 16), 16), :].astype(F32)
        R.dgs[1:2, :] += dg
        R.gh[rows] = dh
        R.nm[me, zh, rows] = dh.astype(BF)

    rs2[3]()
    ag_h[0]()
    rs_m[1]()
    ag_h[1]()
    rs_f[2]()
    tw_o = twin(R.ob)

    @pl.loop(0, 4)
    def _(t):
        rows = owned(t)
        R.ob[zh, rows] = (R.hid[rows] + rs_f[4](rows)).astype(BF)

    rs_f[3]()
    tw_o[0]()
    ag_h[2]()

    @pl.loop(0, 4)
    def _(i):
        zi, ci = lax.div(i, 2), lax.rem(i, 2)
        w = R.wa[:, :, :, :, :, PROJ:ATT].reshape(WIDTH, 256)
        grad = mm(R.nm[i].reshape(128, WIDTH), w)
        logits = jnp.zeros((128, 128), F32)
        for h in (0, 1):
            gate = jax.nn.sigmoid(R.gl[i][:, h : h + 1])
            gr = grad[:, h * 128 : (h + 1) * 128]
            a = R.att[i, :, h * 128 : (h + 1) * 128]
            low = (gr * gate).astype(BF)
            dl = jnp.sum(gr * a, axis=1, keepdims=True) * (gate * (1.0 - gate))
            logits = jnp.where(lanes == h, dl, logits)
            delta = jnp.sum(low.astype(F32) * a, axis=1, keepdims=True)
            R.dox[zi, h, ci, :, 0:128] = low
            R.dox[zi, h, ci, :, 128:256] = three_parts(-delta, lanes)
        R.gsc[i, :, 512:640] = logits.astype(BF)

    R.oacc[...] = jnp.zeros((2, 512, 256), F32)
    row_t = lax.broadcasted_iota(jnp.int32, (256, 512), 1)
    key_t = lax.broadcasted_iota(jnp.int32, (256, 512), 0)
    seen_t = key_t <= lax.rem(row_t, 256)

    def backward(t, groups, diagonal):
        at = tile(t)
        k = R.kv[at + (ALL, ALL, slice(0, 128))].reshape(256, 128)
        v = R.kv[at + (ALL, ALL, slice(128, 256))].reshape(256, 128)
        kx = jnp.concatenate([k, ones], axis=1)
        vx = jnp.concatenate([v, ones], axis=1)
        kt = k.T
        dk = dv = None
        for g in groups:
            q, d = R.qx[g].reshape(512, 256), R.dox[g].reshape(512, 256)
            p = jnp.exp2(mm_tb(kx, q))
            if g == diagonal:
                p = jnp.where(seen_t, p, 0.0)
            ds = (p * mm_tb(vx, d)).astype(BF)
            dvg = mm(p.astype(BF), d[:, 0:128])
            dkg = mm(ds, q[:, 0:128])
            dk, dv = (dkg, dvg) if dk is None else (dk + dkg, dv + dvg)
            dq = mm(kt, ds)
            R.oacc[g, 0:128] += dq[:, 0:256]
            R.oacc[g, 128:256] += dq[:, 256:512]
        R.kv[at + (ALL, ALL, slice(0, 128))] = dk.astype(BF).reshape(2, 128, 128)
        R.kv[at + (ALL, ALL, slice(128, 256))] = dv.astype(BF).reshape(2, 128, 128)

    @pl.loop(0, j)
    def _(t):
        backward(t, (0, 1), None)

    backward(j, (0, 1), 0)
    rs_m[2]()

    @pl.loop(j + 1, j + 16)
    def _(t):
        backward(t, (1,), None)

    backward(j + 16, (1,), 1)

    @pl.loop(j + 17, 32)
    def _(t):
        R.kv[tile(t)] = jnp.zeros((2, 128, 256), BF)

    rs_m[3]()
    rs_k = scatter(R.kv, (R.k_r2, R.k_r1, R.k_q2, R.k_q1), slice(0, 256))
    rs_k[0]()
    rs_m[4]()
    rs_k[1]()
    gb_m = give_back(R.wm, R.wlm)
    gb_m[0]()

    R.dgh[...] = jnp.zeros((8, 128), F32)

    @pl.loop(0, 4)
    def _(i):
        zi, ci = lax.div(i, 2), lax.rem(i, 2)
        for h in (0, 1):
            cols = pl.ds(pl.multiple_of(ci * 128, 128), 128)
            dq = R.oacc[zi, h * 128 : (h + 1) * 128, cols].T * SCALE
            dq = rope_back(dq, R.cos[i], R.sin[i])
            dv, dg = rms_back(R.qraw[i, :, h * 128 : (h + 1) * 128], R.qg[...], dq)
            R.dgh[0:1, :] += dg
            R.gsc[i, :, h * 128 : (h + 1) * 128] = dv.astype(BF)

    rs_k[2]()

    @pl.loop(0, 8)
    def _(n):
        at = (lax.div(n, 4), lax.rem(n, 4), ALL, ALL, ALL, slice(PROJ, ATT))
        cols = pl.ds(pl.multiple_of(n * 256, 256), 256)
        t = R.nm[:, :, :, cols].reshape(512, 256).T
        g = mm(t, R.gated[...].reshape(512, 256))
        R.wa[at] = g.astype(BF).reshape(4, 2, 32, 256)

    rs_k[3]()
    rs_k[4]()

    @pl.loop(0, 4)
    def _(i):
        zi, ci = lax.div(i, 2), lax.rem(i, 2)
        dk = R.kv[zi, y, x, ci, :, 0:128].astype(F32) * LN2
        dk = rope_back(dk, R.cos[i], R.sin[i])
        dv, dg = rms_back(R.kraw[i], R.kg[...], dk)
        R.dgh[1:2, :] += dg
        R.gsc[i, :, 256:384] = dv.astype(BF)
        R.gsc[i, :, 384:512] = R.kv[zi, y, x, ci, :, 128:256]

    @pl.loop(0, 8)
    def _(n):
        w = R.wa[lax.div(n, 4), lax.rem(n, 4), :, :, :, 0:PROJ].reshape(256, PROJ)
        cols, v = spread(n, mm_tb(R.gsc[...].reshape(512, PROJ), w))
        R.pb[:, :, :, cols] = v

    rs3 = reduce_rows(R.pb, R.rsib, R.rz)
    rs3[0]()

    @pl.loop(0, 8)
    def _(n):
        at = (lax.div(n, 4), lax.rem(n, 4), ALL, ALL, ALL, slice(0, PROJ))
        cols = pl.ds(pl.multiple_of(n * 256, 256), 256)
        t = R.xn[:, :, :, cols].reshape(512, 256).T
        g = mm(t, R.gsc[...].reshape(512, PROJ))
        R.wa[at] = g.astype(BF).reshape(4, 2, 32, PROJ)

    rs_a = scatter(R.wa, big, slice(0, ATT))
    rs_a[0]()
    rs3[1]()
    rs_a[1]()
    rs3[2]()
    tw_i = twin(R.ib)

    @pl.loop(0, 4)
    def _(t):
        rows = owned(t)
        v = R.x[pl.ds(pl.multiple_of(zh * 64 + t * 16, 16), 16), :].astype(F32)
        dv, dg = rms_back(v, R.ag[...], rs3[4](rows))
        R.dgs[0:1, :] += dg
        R.ib[zh, rows] = (R.gh[rows] + dv).astype(BF)

    tw_i[0]()
    rs3[3]()

    for r in range(16):
        R.sums[0, r : r + 1, :] = R.dgs[0:1, r * 128 : (r + 1) * 128]
        R.sums[0, 16 + r : 17 + r, :] = R.dgs[1:2, r * 128 : (r + 1) * 128]
    R.sums[0, 32:40, :] = R.dgh[...]
    g_z, g_x, g_y, g_c = Group(3), Group(3), Group(3), Group(1)

    def add_up(g, stage, first, devices):
        for i, d in enumerate(devices):
            g.go(R.sums.at[stage], R.came.at[first + i], d, i)

        def finish():
            v = R.sums[stage]
            for i in range(len(devices)):
                g.got(R.came.at[first + i], i)
                v = v + R.came[first + i]
            R.sums[stage + 1] = v
            g.end()

        return finish

    fin = add_up(g_z, 0, 0, zdev)
    rs_a[2]()
    fin()
    fin = add_up(g_x, 1, 3, xdev)
    rs_a[3]()
    fin()
    fin = add_up(g_y, 2, 6, ydev)
    rs_a[4]()
    gb_a = give_back(R.wa, R.wla)
    gb_a[0]()
    fin()
    fin = add_up(g_c, 3, 9, [sib])

    gb_m[1]()
    for i in range(4):
        at = slice(i * 768, (i + 1) * 768)
        R.o_fg[:, at] = R.wlm[i, :, 0:768].astype(F32)
        R.o_fu[:, at] = R.wlm[i, :, 768:1536].astype(F32)
        R.o_fd[:, at] = R.wlm[i, :, 1536:2304].astype(F32)
    tw_o[1]()
    R.o_out[...] = R.ob[...].reshape(128, WIDTH)
    fin()
    R.o_gain[...] = R.sums[4]
    tw_i[1]()
    R.o_in[...] = R.ib[...].reshape(128, WIDTH)
    gb_a[1]()
    gates = jnp.zeros((32, 8), F32)
    for i in range(4):
        R.o_q[:, i * 256 : (i + 1) * 256] = R.wla[i, :, 0:256].astype(F32)
        R.o_k[:, i * 128 : (i + 1) * 128] = R.wla[i, :, 256:384].astype(F32)
        R.o_v[:, i * 128 : (i + 1) * 128] = R.wla[i, :, 384:512].astype(F32)
        R.o_o[:, i * 256 : (i + 1) * 256] = R.wla[i, :, 640:896].astype(F32)
        pick = select(lambda r, q, i=i: (q == r + 2 * i) & (r < 2), (128, 8))
        gates = gates + mm(R.wla[i, :, 512:640], pick)
    R.o_g[...] = gates
    for g in (ag_x, ag_h):
        g[3]()
    gb_m[2]()
    gb_a[2]()
    assert count[0] == COPIES, count


INPUTS = [
    *("x", "ct", "ag", "qg", "kg", "fgain"),
    *("qw", "kw", "vw", "gw", "ow", "fg", "fu", "fd"),
    *("cos", "sin"),
]
OUTPUTS = [
    ("o_out", (128, WIDTH), BF),
    ("o_in", (128, WIDTH), BF),
    ("o_gain", (40, 128), F32),
    ("o_q", (32, 1024), F32),
    ("o_k", (32, 512), F32),
    ("o_v", (32, 512), F32),
    ("o_g", (32, 8), F32),
    ("o_o", (32, 1024), F32),
    ("o_fg", (32, 3072), F32),
    ("o_fu", (32, 3072), F32),
    ("o_fd", (32, 3072), F32),
]
SCRATCH = [
    ("wla", (4, 32, ATT), BF),
    ("wlm", (4, 32, 2304), BF),
    ("wa", (2, 4, 4, 2, 32, ATT), BF),
    ("wm", (2, 4, 4, 2, 32, 2304), BF),
    ("kv", (2, 4, 4, 2, 128, 256), BF),
    ("xn", (4, 2, 64, WIDTH), BF),
    ("cot", (4, 2, 64, WIDTH), BF),
    ("nm", (4, 2, 64, WIDTH), BF),
    ("qraw", (4, 128, 256), F32),
    ("kraw", (4, 128, 128), F32),
    ("gl", (4, 128, 128), F32),
    ("qx", (2, 2, 2, 128, 256), BF),
    ("dox", (2, 2, 2, 128, 256), BF),
    ("oacc", (2, 512, 256), F32),
    ("att", (4, 128, 256), F32),
    ("gated", (4, 128, 256), BF),
    ("gsc", (4, 128, PROJ), BF),
    ("act", (3, 512, 768), BF),
    ("hid", (64, WIDTH), F32),
    ("gh", (64, WIDTH), F32),
    ("dgs", (2, WIDTH), F32),
    ("dgh", (8, 128), F32),
    ("pb", (4, 2, 64, WIDTH), BF),
    ("pb2", (4, 2, 64, WIDTH), BF),
    ("rsib", (2, 2, 64, WIDTH), BF),
    ("rsib2", (2, 2, 64, WIDTH), BF),
    ("rz", (3, 64, WIDTH), BF),
    ("rz2", (3, 64, WIDTH), BF),
    ("m_r2", (2, 2, 4, 32, 2304), BF),
    ("m_r1", (2, 2, 4, 2, 32, 2304), BF),
    ("m_q2", (2, 2, 1, 32, 2304), BF),
    ("m_q1", (2, 2, 1, 2, 32, 2304), BF),
    ("k_r2", (2, 2, 4, 128, 256), BF),
    ("k_r1", (2, 2, 4, 2, 128, 256), BF),
    ("k_q2", (2, 2, 1, 128, 256), BF),
    ("k_q1", (2, 2, 1, 2, 128, 256), BF),
    ("ob", (2, 64, WIDTH), BF),
    ("ib", (2, 64, WIDTH), BF),
    ("sums", (5, 40, 128), F32),
    ("came", (10, 40, 128), F32),
]
COPIES = 164


def kernel(*refs):
    names = INPUTS + [o[0] for o in OUTPUTS] + [v[0] for v in SCRATCH] + ["send", "recv", "free"]
    body(SimpleNamespace(**dict(zip(names, refs))))


def per_device(
    inputs,
    attention_gain,
    query_weight,
    key_matrix,
    value_matrix,
    gate_weight,
    query_gain,
    key_gain,
    out_weight,
    feed_gain,
    feed_gate,
    feed_up,
    feed_down,
    cotangent,
):
    place = lax.axis_index("seq")
    run = lax.rem(lax.div(place, 2), 16)
    half = jnp.arange(4, dtype=jnp.int32)[:, None]
    row = jnp.arange(128, dtype=jnp.int32)[None, :]
    positions = (half // 2) * 4096 + run * 256 + (half % 2) * 128 + row
    inverse = ROPE_BASE ** (-(jnp.arange(HEAD // 2, dtype=F32) * 2.0) / HEAD)
    angles = positions.astype(F32)[:, :, None] * inverse
    cos, sin = jnp.cos(angles), jnp.sin(angles)
    cos = jnp.concatenate([cos, cos], axis=-1)
    sin = jnp.concatenate([-sin, sin], axis=-1)
    vmem = pl.BlockSpec(memory_space=pltpu.VMEM)
    out = pl.pallas_call(
        kernel,
        out_shape=[jax.ShapeDtypeStruct(shape, kind) for _, shape, kind in OUTPUTS],
        in_specs=[vmem] * len(INPUTS),
        out_specs=[vmem] * len(OUTPUTS),
        scratch_shapes=[pltpu.VMEM(shape, kind) for _, shape, kind in SCRATCH]
        + [pltpu.SemaphoreType.DMA((COPIES,)), pltpu.SemaphoreType.DMA((COPIES,))]
        + [pltpu.SemaphoreType.REGULAR],
        compiler_params=pltpu.CompilerParams(
            collective_id=0, has_side_effects=True, vmem_limit_bytes=63 * 2**20
        ),
        name="block",
    )(
        inputs,
        cotangent,
        attention_gain.reshape(1, WIDTH),
        query_gain.reshape(1, HEAD),
        key_gain.reshape(1, HEAD),
        feed_gain.reshape(1, WIDTH),
        query_weight,
        key_matrix,
        value_matrix,
        gate_weight,
        out_weight.T,
        feed_gate,
        feed_up,
        feed_down.T,
        cos,
        sin,
    )
    output, grad_inputs, gains, gq, gk, gv, gg, go, gfg, gfu, gfd = out
    own = lax.dynamic_slice_in_dim(gains[:32].reshape(2, WIDTH), place * 32, 32, 1)
    return (
        output,
        grad_inputs,
        own[0],
        gq,
        gk,
        gv,
        gg,
        gains[32],
        gains[33],
        go.T,
        own[1],
        gfg,
        gfu,
        gfd.T,
    )


def solution(mesh):
    seq, both, turned = P("seq", None), P("seq", "grp"), P("grp", "seq")
    in_specs = (seq, P(), both, both, both, both, P(), P(), turned, P(), both, both, turned, seq)
    out_specs = (
        seq, seq, P("seq"), both, both, both, both, P(), P(), turned, P("seq"), both, both, turned,
    )
    return jax.shard_map(
        per_device, mesh=mesh, in_specs=in_specs, out_specs=out_specs, check_vma=False
    )
```

time: 4390 us -> 320 us (0.07)
  waiting for transfers between devices: 3720 us -> 0 us
  blocking collectives: 431 us -> 0 us
  Pallas kernels: 0 us -> 304 us
  matrix products: 135 us -> 0 us
    reduce_scatter x9 -> x0, waiting for transfers between devices: 2530 us -> none  [the longest x1 376 us: per_device(): lax.psum_scatter(grad_keys, 'seq', scatter_dimension=0, tiled=True)]
    all_gather x9 -> x0, waiting for transfers between devices: 896 us -> none  [the longest x1 118 us: per_device(): lax.all_gather(keys_local, 'seq', axis=0, tiled=True)]
    pallas_call x0 -> x1, Pallas kernels: none -> 304 us  [per_device(): pl.pallas_call(kernel, out_shape=[jax.ShapeDtypeStruct(shape, kind) for _...]
    unnamed x1 -> x0, blocking collectives: 270 us -> none
    unnamed x23 -> x0, waiting for transfers between devices: 234 us -> none
    dot_general x29 -> x0, matrix products: 129 us -> none  [the longest x7 48.9 us: inner(): lax.dot_general(left_side, right_side, (((0,), (0,)), ((), ())), preferre...]
    psum x1 -> x0, blocking collectives: 81.5 us -> none  [per_device(): gain_totals = lax.psum((grad_query_gain, grad_key_gain), ('seq', 'grp'))]
    all_gather x1 -> x0, blocking collectives: 79.7 us -> none  [per_device(): lax.all_gather(gate_weight, 'seq', axis=0, tiled=True)]
  transfers between devices with their start and end apart: 22 -> 0, of which waited for: 20 -> 0; matrix products, arithmetic and copies ran while one was open for 3% -> 0% of each run, Pallas kernels for 0% -> 0%
where the time goes in v1:
time: 320 us; the launch traced here: 319 us
  Pallas kernels  304 us (95%)
  local copies, waits for them, and re-layouts  12.4 us (4%)
    pallas_call x1, Pallas kernels, per_device(): pl.pallas_call(kernel, out_shape=[jax.ShapeDtypeStruct(shape, kind) for _...  304 us
    unnamed x33, local copies, waits for them, and re-layouts  11.2 us

profile of v1, /device:TPU:1, one launch (start us, length us, event | category | flops | bytes accessed | tf_op | source)
XLA Modules:
  0.0 319.4 jit_solution(1574245615489106771)
XLA Ops:
  0.7 0.1 add_convert_fusion
  0.8 0.6 copy-done.10
  1.4 0.7 copy.28.refs_9_
  2.0 1.0 fusion
  3.0 1.0 pad_maximum_fusion
  4.0 304.3 %block.1 = (bf16[128,2048]{1,0:T(8,128)(2,1)}, bf16[128,2048]{1,0:T(8,128)(2,1)}, f32[40,128]{1,0:T(8,128)}, f32[32,1024]{1,0:T(8,128)}, f32[32,512]{1,0:T(8,128...) custom-call(bf16[128,2048]{1,0:T(8,128)(2,1)} %refs_0_.1, ...), custom_call_target="tpu_custom_call" | custom-call | tf_op jit(solution)/shard_map/block/pallas_call | solution.py:944
  308.3 0.7 copy-done.9
  309.0 0.5 slice_bitcast_fusion.1
  309.6 0.1 constant_dynamic-slice_fusion
  309.6 0.5 slice_bitcast_fusion
  310.2 0.1 copy-done.8
  310.3 0.7 copy.29
  310.9 1.9 copy.39
  312.9 0.8 copy.40
  313.7 0.1 copy-done.5
  313.8 0.7 copy.41
  314.5 0.6 copy.42
  315.1 0.6 copy.43
  315.8 0.7 copy.44
  316.4 0.7 copy.45
  317.2 0.4 copy-done.2
  317.6 0.7 copy.46
  318.3 0.4 copy-done.1
  318.7 0.7 copy.47
  (20 shorter events, 0.1 us)
Async XLA Ops:
  0.7 0.7 copy-start.10
  308.3 0.7 copy-start.9
  309.6 0.7 copy-start.8
  310.9 1.9 copy-start
  312.9 1.0 copy-start.5
  312.9 1.6 copy-start.7
  312.9 2.2 copy-start.6
  312.9 2.9 copy-start.4
  313.8 2.6 copy-start.3
  316.4 1.1 copy-start.2
  317.6 1.1 copy-start.1

commit v2 on v1

--- a/solution.py
+++ b/solution.py
@@ -90,7 +90,8 @@
     ydev = [dev(z, up(y, k), x, c) for k in (1, 3, 2)]
 
     barrier = pltpu.get_barrier_semaphore()
-    greet = [sib, diag] + zdev + xdev + ydev
+    zsib = [dev(v, y, x, 1 - c) for v in zs]
+    greet = [sib] + zdev + zsib + xdev + ydev
     for d in greet:
         pl.semaphore_signal(barrier, inc=1, device_id=d, device_id_type=MESH)
 
@@ -174,26 +175,31 @@
     )
 
     def gather_ring(buf, a):
-        g, p = Group(4), a.pos
+        g, p = Group(6), a.pos
+        left, right, across = up(p, 3), up(p, 1), up(p, 2)
+
+        def half(q, h):
+            return buf.at[a.half(q, h)]
 
         def s1():
-            mine = buf.at[a.full(p)]
-            g.go(mine, mine, a.dev[0], 0)
-            g.go(mine, mine, a.dev[1], 1)
+            for i, (h, d) in enumerate(((0, 0), (1, 1), (1, 0), (0, 1))):
+                g.go(half(p, h), half(p, h), a.dev[d], i)
 
         def s2():
-            g.got(buf.at[a.full(up(p, 3))], 0)
-            low = buf.at[a.half(up(p, 3), 0)]
-            g.go(low, low, a.dev[0], 2)
-            g.got(buf.at[a.full(up(p, 1))], 1)
-            high = buf.at[a.half(up(p, 1), 1)]
-            g.go(high, high, a.dev[1], 3)
+            g.got(half(left, 0), 0)
+            g.go(half(left, 0), half(left, 0), a.dev[0], 4)
+            g.got(half(right, 1), 1)
+            g.go(half(right, 1), half(right, 1), a.dev[1], 5)
 
         def s3():
-            g.got(buf.at[a.half(up(p, 2), 0)], 2)
-            g.got(buf.at[a.half(up(p, 2), 1)], 3)
-
-        return s1, s2, s3, g.end
+            g.got(half(left, 1), 2)
+            g.got(half(right, 0), 3)
+
+        def s4():
+            g.got(half(across, 0), 4)
+            g.got(half(across, 1), 5)
+
+        return s1, s2, s3, s4, g.end
 
     def gather(buf):
         one = [gather_ring(buf, a_x), gather_ring(buf, b_y)]
@@ -210,6 +216,7 @@
         def t3():
             for r, q in zip(one, two):
                 r[2]()
+                r[3]()
                 q[0]()
 
         def t4():
@@ -219,18 +226,31 @@
         def t5():
             for r in two:
                 r[2]()
+
+        def t6():
+            for r in two:
+                r[3]()
             for r in one + two:
-                r[3]()
-
-        return t1, t2, t3, t4, t5
-
-    def reduce_ring(buf, a, r2, r1, cs):
-        g, p, k = Group(4), a.pos, a.k
-
-        def slot(ref, i):
-            if k == 1:
-                return ref.at[(i, 0) + (ALL,) * (len(ref.shape) - 3) + (cs,)]
-            return ref.at[(i,) + (ALL,) * (len(ref.shape) - 2) + (cs,)]
+                r[4]()
+
+        return t1, t2, t3, t4, t5, t6
+
+    def reduce_ring(buf, a, r2, r1, cs, bs):
+        g, p, k = Group(6), a.pos, a.k
+        first = ALL if k == 4 else 0
+
+        def half(q, h):
+            at = a.half(q, h)
+            return buf.at[at + (ALL,) * (5 - len(at)) + (cs,)]
+
+        def elem(q, n, h):
+            return a.elem(q, n, h) + (ALL, cs)
+
+        def far(i):
+            return r2.at[i, first, :, bs]
+
+        def near(i, h):
+            return r1.at[i, first, h, :, bs]
 
         def loop(fn):
             if k == 1:
@@ -239,132 +259,180 @@
                 pl.loop(0, k)(fn)
 
         def s1():
-            g.go(buf.at[a.half(up(p, 2), 0)], slot(r2, 0), a.dev[0], 0)
-            g.go(buf.at[a.half(up(p, 2), 1)], slot(r2, 1), a.dev[1], 1)
-
-        def s2():
-            for i, step in ((0, 1), (1, 3)):
-                g.got(slot(r2, i), i)
-                to = up(p, step)
-
-                def add(q, i=i, to=to):
-                    at = a.elem(to, q, i)
-                    buf[at] = buf[at] + r2[i, q, :, cs]
-
-                loop(add)
-                g.go(buf.at[a.full(to)], slot(r1, i), a.dev[i], 2 + i)
+            for i in (0, 1):
+                g.go(half(up(p, 2), i), far(i), a.dev[i], i)
+
+        def direct(i):
+            g.go(half(up(p, 1 + 2 * i), 1 - i), near(i, 1 - i), a.dev[i], 2 + i)
+
+        def s2(i):
+            g.got(far(i), i)
+            to = up(p, 1 + 2 * i)
+
+            def add(n):
+                at = elem(to, n, i)
+                buf[at] = buf[at] + r2[i, n, :, bs]
+
+            loop(add)
+            g.go(half(to, i), near(i, i), a.dev[i], 4 + i)
 
         def s3():
-            g.got(slot(r1, 0), 2)
-            g.got(slot(r1, 1), 3)
-
-            def add(q):
+            for i in (0, 1):
+                g.got(near(i, 1 - i), 2 + i)
+                g.got(near(i, i), 4 + i)
+
+            def add(n):
                 for h in (0, 1):
-                    at = a.elem(p, q, h)
+                    at = elem(p, n, h)
                     total = (
                         buf[at].astype(F32)
-                        + r1[0, q, h, :, cs].astype(F32)
-                        + r1[1, q, h, :, cs].astype(F32)
+                        + r1[0, n, h, :, bs].astype(F32)
+                        + r1[1, n, h, :, bs].astype(F32)
                     )
                     buf[at] = total.astype(BF)
 
             loop(add)
 
-        return s1, s2, s3, g.end
-
-    def scatter(buf, bufs, cs):
+        return s1, direct, s2, s3, g.end
+
+    def scatter(buf, bufs, cs, bs=None):
+        bs = cs if bs is None else bs
         one = [
-            reduce_ring(buf, a_y, bufs[0].at[0], bufs[1].at[0], cs),
-            reduce_ring(buf, b_x, bufs[0].at[1], bufs[1].at[1], cs),
+            reduce_ring(buf, a_y, bufs[0].at[0], bufs[1].at[0], cs, bs),
+            reduce_ring(buf, b_x, bufs[0].at[1], bufs[1].at[1], cs, bs),
         ]
         two = [
-            reduce_ring(buf, a_x, bufs[2].at[0], bufs[3].at[0], cs),
-            reduce_ring(buf, b_y, bufs[2].at[1], bufs[3].at[1], cs),
+            reduce_ring(buf, a_x, bufs[2].at[0], bufs[3].at[0], cs, bs),
+            reduce_ring(buf, b_y, bufs[2].at[1], bufs[3].at[1], cs, bs),
         ]
 
-        def t1():
+        def t0():
             for r in one:
                 r[0]()
 
-        def t2():
+        def t1(i):
             for r in one:
-                r[1]()
+                r[1](i)
+
+        def t2(i):
+            for r in one:
+                r[2](i)
 
         def t3():
             for r, q in zip(one, two):
-                r[2]()
+                r[3]()
                 q[0]()
+                q[1](0)
+                q[1](1)
 
         def t4():
-            for r in two:
-                r[1]()
+            for i in (0, 1):
+                for r in two:
+                    r[2](i)
 
         def t5():
             for r in two:
-                r[2]()
+                r[3]()
             for r in one + two:
-                r[3]()
-
-        return t1, t2, t3, t4, t5
+                r[4]()
+
+        def start():
+            t0()
+            t1(0)
+            t1(1)
+
+        def onward():
+            t2(0)
+            t2(1)
+
+        return SimpleNamespace(t0=t0, t1=t1, t2=t2, t3=t3, t4=t4, t5=t5, start=start, onward=onward)
+
+    def place(zz, cc):
+        return (lax.rem(zz, 2) * 2 + cc, lax.div(zz, 2))
+
+    half_rows = (slice(0, 32), slice(32, 64))
 
     def reduce_rows(pb, rsib, rz):
-        g = Group(5)
+        g = Group(8)
+
+        def mine(zz, h):
+            return pb.at[place(zz, c) + (half_rows[h],)]
 
         def s0():
             for t in (0, 1):
                 g.go(pb.at[t * 2 + 1 - c], rsib.at[t], sib, t)
 
         def s1():
-            for t in (0, 1):
-                g.got(rsib.at[t], t)
-
-                def add(h, t=t):
-                    pb[t * 2 + c, h] = pb[t * 2 + c, h] + rsib[t, h]
-
-                pl.loop(0, 2)(add)
-            for i in range(3):
-                zz = zs[i]
-                src = pb.at[lax.rem(zz, 2) * 2 + c, lax.div(zz, 2)]
-                g.go(src, rz.at[i], zdev[i], 2 + i)
+            g.got(rsib.at[0], 0)
+            g.got(rsib.at[1], 1)
+
+            def add(zz):
+                at = place(zz, c)
+                pb[at] = pb[at] + rsib[lax.rem(zz, 2), lax.div(zz, 2)]
+
+            add(zs[2])
+            for i in (0, 1):
+                g.go(mine(zs[2], i), rz.at[2, half_rows[i]], zdev[i], 2 + i)
+            for i in (0, 1):
+                add(zs[i])
+                g.go(mine(zs[i], 1 - i), rz.at[i, half_rows[1 - i]], zdev[i], 4 + i)
+            add(z)
 
         def s2():
-            for i in range(3):
-                g.got(rz.at[i], 2 + i)
+            for i in (0, 1):
+                rows = half_rows[i]
+                g.got(rz.at[2, rows], 2 + i)
+                at = place(zs[i], c) + (rows,)
+                pb[at] = pb[at] + rz[2, rows]
+                g.go(mine(zs[i], i), rz.at[i, rows], zdev[i], 6 + i)
+
+        def s3():
+            for i in (0, 1):
+                g.got(rz.at[i, half_rows[1 - i]], 4 + i)
+                g.got(rz.at[i, half_rows[i]], 6 + i)
 
         def total(rows):
             v = pb[me, zh, rows].astype(F32)
-            for i in range(3):
-                v = v + rz[i, rows].astype(F32)
-            return v
-
-        return s0, s1, s2, g.end, total
+            return v + rz[0, rows].astype(F32) + rz[1, rows].astype(F32)
+
+        return SimpleNamespace(s0=s0, s1=s1, s2=s2, s3=s3, end=g.end, total=total)
 
     def gather_rows(buf):
-        g = Group(7)
-
-        def place(zz, cc):
-            return buf.at[lax.rem(zz, 2) * 2 + cc, lax.div(zz, 2)]
+        g = Group(10)
+
+        def at(zz, h):
+            return buf.at[place(zz, c) + (half_rows[h],)]
 
         def s0():
-            mine = buf.at[me, zh]
-            for i in range(3):
-                g.go(mine, mine, zdev[i], i)
-            g.go(mine, mine, sib, 3)
-
-        came = [zs[1], zs[0], zs[2]]
+            for i, (h, d) in enumerate(((0, 0), (1, 1), (1, 0), (0, 1))):
+                g.go(at(z, h), at(z, h), zdev[d], i)
+            own = buf.at[place(z, c)]
+            g.go(own, own, sib, 6)
 
         def s1():
-            for i in range(3):
-                at = place(came[i], c)
-                g.got(at, i)
-                g.go(at, at, sib, 4 + i)
+            g.got(at(zs[1], 0), 0)
+            g.go(at(zs[1], 0), at(zs[1], 0), zdev[0], 4)
+            g.got(at(zs[0], 1), 1)
+            g.go(at(zs[0], 1), at(zs[0], 1), zdev[1], 5)
 
         def s2():
-            g.got(place(z, 1 - c), 3)
-            for i in range(3):
-                g.got(place(came[i], 1 - c), 4 + i)
-
-        return s0, s1, s2, g.end
+            def hand_on(zz, i):
+                whole = buf.at[place(zz, c)]
+                g.go(whole, whole, sib, i)
+
+            g.got(at(zs[1], 1), 2)
+            hand_on(zs[1], 7)
+            g.got(at(zs[0], 0), 3)
+            hand_on(zs[0], 8)
+            g.got(at(zs[2], 0), 4)
+            g.got(at(zs[2], 1), 5)
+            hand_on(zs[2], 9)
+
+        def s3():
+            for i, zz in ((6, z), (7, zs[1]), (8, zs[0]), (9, zs[2])):
+                g.got(buf.at[place(zz, 1 - c)], i)
+
+        return SimpleNamespace(s0=s0, s1=s1, s2=s2, s3=s3, end=g.end)
 
     def gather_blocks(buf):
         g = Group(5)
@@ -405,11 +473,8 @@
         R.wla[i, :, 384:512] = R.vw[:, i * 128 : (i + 1) * 128]
         pick = select(lambda r, q, i=i: (r == q + 2 * i) & (q < 2), (8, 128))
         R.wla[i, :, 512:640] = mm(R.gw[...], pick).astype(BF)
-        R.wla[i, :, 640:896] = R.ow[:, i * 256 : (i + 1) * 256]
-    ex_a = exchange(R.wa, R.wla)
-    ag_a = gather(R.wa)
-    ex_m = exchange(R.wm, R.wlm)
-    ag_m = gather(R.wm)
+    ex_a, ex_o, ex_m = exchange(R.wa, R.wla), exchange(R.wo, R.wlo), exchange(R.wm, R.wlm)
+    ag_a, ag_o, ag_m = gather(R.wa), gather(R.wo), gather(R.wm)
     ag_x = gather_blocks(R.xn)
     ag_c = gather_blocks(R.cot)
     ag_kv = gather(R.kv)
@@ -425,28 +490,31 @@
 
     ag_x[0]()
     for i in range(4):
+        R.wlo[i] = R.ow[:, i * 256 : (i + 1) * 256]
         R.wlm[i, :, 0:768] = R.fg[:, i * 768 : (i + 1) * 768]
         R.wlm[i, :, 768:1536] = R.fu[:, i * 768 : (i + 1) * 768]
         R.wlm[i, :, 1536:2304] = R.fd[:, i * 768 : (i + 1) * 768]
     R.cot[me] = R.ct[...].reshape(2, 64, WIDTH)
     ex_a[1]()
     ag_a[0]()
+    ag_a[1]()
     ag_x[1]()
-    ag_a[1]()
+    ag_a[2]()
+    ex_o[0]()
     ex_m[0]()
-    ag_c[0]()
-    ag_a[2]()
     ag_x[2]()
     ag_a[3]()
-    ag_c[1]()
+    ex_o[1]()
+    ag_o[0]()
+    ag_a[4]()
     ex_m[1]()
-    ag_a[4]()
     ag_m[0]()
+    ag_a[5]()
 
     @pl.loop(0, 4)
     def _(i):
         zi, ci = lax.div(i, 2), lax.rem(i, 2)
-        w = R.wa[:, :, :, :, :, 0:PROJ].reshape(WIDTH, PROJ)
+        w = R.wa[...].reshape(WIDTH, PROJ)
         raw = mm(R.xn[i].reshape(128, WIDTH), w)
         cos, sin = R.cos[i], R.sin[i]
         R.qraw[i] = raw[:, 0:256]
@@ -462,25 +530,15 @@
         R.kv[zi, y, x, ci, :, 128:256] = raw[:, 384:512].astype(BF)
 
     ag_kv[0]()
-    ag_m[1]()
-    ag_kv[1]()
-    ag_kv[2]()
-    ag_kv[3]()
-    ag_kv[4]()
-    ag_m[2]()
+    ag_c[0]()
 
     ones = jnp.ones((256, 128), BF)
     key_i = lax.broadcasted_iota(jnp.int32, (512, 256), 1)
     row_i = lax.broadcasted_iota(jnp.int32, (512, 256), 0)
     seen = key_i <= lax.rem(row_i, 256)
-
-    def tile(t):
-        return (lax.div(t, 16), lax.rem(lax.div(t, 4), 4), lax.rem(t, 4))
-
     R.oacc[...] = jnp.zeros((2, 512, 256), F32)
 
-    def forward(t, groups, diagonal):
-        at = tile(t)
+    def forward(at, groups, diagonal):
         k = R.kv[at + (ALL, ALL, slice(0, 128))].reshape(256, 128)
         v = R.kv[at + (ALL, ALL, slice(128, 256))].reshape(256, 128)
         v = jnp.concatenate([v, ones], axis=1)
@@ -490,18 +548,58 @@
                 p = jnp.where(seen, p, 0.0)
             R.oacc[g] += mm(p.astype(BF), v)
 
-    @pl.loop(0, j)
-    def _(t):
-        forward(t, (0, 1), None)
-
-    forward(j, (0, 1), 0)
-
-    @pl.loop(j + 1, j + 16)
-    def _(t):
-        forward(t, (1,), None)
-
-    forward(j + 16, (1,), 1)
-    ag_m[3]()
+    def tile_pair(fn, empty, at0, at1):
+        t0, t1 = at0[0] * 4 + at0[1], at1[0] * 4 + at1[1]
+
+        @pl.when(t0 < j)
+        def _():
+            fn((0,) + at0, (0, 1), None)
+
+        @pl.when(t0 > j)
+        def _():
+            fn((0,) + at0, (1,), None)
+
+        @pl.when(t1 < j)
+        def _():
+            fn((1,) + at1, (1,), None)
+
+        if empty is not None:
+
+            @pl.when(t1 > j)
+            def _():
+                empty((1,) + at1)
+
+    def near(fn, empty=None):
+        @pl.loop(1, 4)
+        def _(k):
+            tile_pair(fn, empty, (y, up(x, k)), (up(y, k), x))
+
+    def side(fn, a, empty=None):
+        @pl.loop(0, 4)
+        def _(k):
+            tile_pair(fn, empty, (up(y, a), k), (k, up(x, a)))
+
+    ag_o[1]()
+    forward((0, y, x), (0, 1), 0)
+    forward((1, y, x), (1,), 1)
+    ag_kv[1]()
+    ag_m[1]()
+    ag_kv[2]()
+    ag_o[2]()
+    near(forward)
+    ag_c[1]()
+    ag_kv[3]()
+    ag_o[3]()
+    ag_kv[4]()
+    ag_m[2]()
+    @pl.loop(0, 2)
+    def _(k):
+        side(forward, 1 + 2 * k)
+
+    ag_kv[5]()
+    side(forward, 2)
+    ag_o[4]()
+    ag_o[5]()
 
     lanes = lax.broadcasted_iota(jnp.int32, (128, 128), 1)
 
@@ -521,17 +619,27 @@
         cols = pl.ds(pl.multiple_of(n * 256, 256), 256)
         return cols, value.reshape(4, 2, 64, 256).astype(BF)
 
-    @pl.loop(0, 8)
-    def _(n):
-        w = R.wa[lax.div(n, 4), lax.rem(n, 4), :, :, :, PROJ:ATT].reshape(256, 256)
-        cols, v = spread(n, mm_tb(R.gated[...].reshape(512, 256), w))
-        R.pb[:, :, :, cols] = v
-
     rs1 = reduce_rows(R.pb, R.rsib, R.rz)
     ag_n = gather_rows(R.nm)
-    rs1[0]()
-    rs1[1]()
-    rs1[2]()
+
+    def project(cc):
+        rows = jnp.concatenate([R.gated[cc], R.gated[2 + cc]], axis=0)
+
+        @pl.loop(0, 8)
+        def _(n):
+            w = R.wo[lax.div(n, 4), lax.rem(n, 4)].reshape(256, 256)
+            cols = pl.ds(pl.multiple_of(n * 256, 256), 256)
+            v = mm_tb(rows, w).astype(BF).reshape(2, 2, 64, 256)
+            R.pb[cc, :, :, cols] = v[0]
+            R.pb[2 + cc, :, :, cols] = v[1]
+
+    project(1 - c)
+    rs1.s0()
+    project(c)
+    rs1.s1()
+    rs1.s2()
+    ag_m[3]()
+    rs1.s3()
 
     def owned(t):
         return pl.ds(pl.multiple_of(t * 16, 16), 16)
@@ -540,18 +648,20 @@
     def _(t):
         rows = owned(t)
         v = R.x[pl.ds(pl.multiple_of(zh * 64 + t * 16, 16), 16), :].astype(F32)
-        v = v + rs1[4](rows)
+        v = v + rs1.total(rows)
         R.hid[rows] = v
         R.nm[me, zh, rows] = (v * rms_scale(v) * R.fgain[...]).astype(BF)
 
-    rs1[3]()
-    ex_a[2]()
-    ex_m[2]()
-    ag_n[0]()
+    rs1.end()
+    for g in (ex_a, ex_o, ex_m):
+        g[2]()
+    ag_n.s0()
     ag_c[2]()
+    ag_n.s1()
+    ag_n.s2()
     ag_m[4]()
-    ag_n[1]()
-    ag_n[2]()
+    ag_m[5]()
+    ag_n.s3()
 
     @pl.loop(0, 3)
     def _(n):
@@ -571,82 +681,92 @@
         R.act[1, :, cols] = (grad * silu).astype(BF)
         R.act[2, :, cols] = (silu * upper).astype(BF)
 
+    def block(n):
+        return (lax.div(n, 4), lax.rem(n, 4), ALL, ALL, ALL)
+
+    def turned(ref, n):
+        cols = pl.ds(pl.multiple_of(n * 256, 256), 256)
+        return ref[:, :, :, cols].reshape(512, 256).T
+
+    big = (R.m_r2, R.m_r1, R.m_q2, R.m_q1)
+    rs_d = scatter(R.ga, big, slice(0, 768))
+    rs_m = scatter(R.wm, big, slice(0, 1536), slice(768, 2304))
+
     @pl.loop(0, 8)
     def _(n):
-        at = (lax.div(n, 4), lax.rem(n, 4), ALL, ALL, ALL)
+        g = mm(turned(R.cot, n), R.act[2])
+        R.ga[block(n) + (slice(0, 768),)] = g.astype(BF).reshape(4, 2, 32, 768)
+
+    rs_d.start()
+
+    @pl.loop(0, 8)
+    def _(n):
+        at = block(n)
         v = mm_tb(R.act[0], R.wm[at + (slice(0, 768),)].reshape(256, 768))
         v = v + mm_tb(R.act[1], R.wm[at + (slice(768, 1536),)].reshape(256, 768))
         cols, v = spread(n, v)
         R.pb[:, :, :, cols] = v
 
     rs2 = reduce_rows(R.pb, R.rsib, R.rz)
-    rs_f = reduce_rows(R.pb2, R.rsib2, R.rz2)
-    rs2[0]()
+    rs_f = reduce_rows(R.pb2, R.rsib, R.rz)
+    rs2.s0()
+
+    def feed_weights(n):
+        at = block(n)
+        t = turned(R.nm, n)
+        R.wm[at + (slice(0, 768),)] = mm(t, R.act[0]).astype(BF).reshape(4, 2, 32, 768)
+        R.wm[at + (slice(768, 1536),)] = mm(t, R.act[1]).astype(BF).reshape(4, 2, 32, 768)
+
+    pl.loop(0, 4)(feed_weights)
+    rs2.s1()
+    rs_d.onward()
+    pl.loop(4, 8)(feed_weights)
+    rs2.s2()
+
+    def tell(devices, sem):
+        for d in devices:
+            pl.semaphore_signal(sem, inc=1, device_id=d, device_id_type=MESH)
+
+    group = [sib] + zdev
+    ring = xdev[:2] + ydev[:2]
+    ag_n.end()
+    tell(group, R.free.at[0])
+    ag_h = gather_rows(R.nm)
+    rs_m.start()
 
     @pl.loop(0, 8)
     def _(n):
-        at = (lax.div(n, 4), lax.rem(n, 4), ALL, ALL, ALL)
-        w = R.wm[at + (slice(1536, 2304),)].reshape(256, 768)
+        w = R.wm[block(n) + (slice(1536, 2304),)].reshape(256, 768)
         cols, v = spread(n, mm_tb(R.act[2], w))
         R.pb2[:, :, :, cols] = v
 
-    rs2[1]()
-    rs_f[0]()
-
-    @pl.loop(0, 8)
-    def _(n):
-        at = (lax.div(n, 4), lax.rem(n, 4), ALL, ALL, ALL)
-        cols = pl.ds(pl.multiple_of(n * 256, 256), 256)
-        t = R.nm[:, :, :, cols].reshape(512, 256).T
-        R.wm[at + (slice(0, 768),)] = mm(t, R.act[0]).astype(BF).reshape(4, 2, 32, 768)
-        R.wm[at + (slice(768, 1536),)] = mm(t, R.act[1]).astype(BF).reshape(4, 2, 32, 768)
-        t = R.cot[:, :, :, cols].reshape(512, 256).T
-        R.wm[at + (slice(1536, 2304),)] = mm(t, R.act[2]).astype(BF).reshape(4, 2, 32, 768)
-
-    ag_n[3]()
-    for d in [sib] + zdev:
-        pl.semaphore_signal(R.free, inc=1, device_id=d, device_id_type=MESH)
-
-    big = (R.m_r2, R.m_r1, R.m_q2, R.m_q1)
-    rs_m = scatter(R.wm, big, slice(0, 2304))
-    ag_h = gather_rows(R.nm)
-    rs_m[0]()
-    rs_f[1]()
-    rs2[2]()
     R.dgs[...] = jnp.zeros((2, WIDTH), F32)
     ag_c[3]()
-    pl.semaphore_wait(R.free, 4)
+    rs2.s3()
+    pl.semaphore_wait(R.free.at[0], 4)
 
     @pl.loop(0, 4)
     def _(t):
         rows = owned(t)
-        dv, dg = rms_back(R.hid[rows], R.fgain[...], rs2[4](rows))
+        dv, dg = rms_back(R.hid[rows], R.fgain[...], rs2.total(rows))
         dh = dv + R.ct[pl.ds(pl.multiple_of(zh * 64 + t * 16, 16), 16), :].astype(F32)
         R.dgs[1:2, :] += dg
         R.gh[rows] = dh
         R.nm[me, zh, rows] = dh.astype(BF)
 
-    rs2[3]()
-    ag_h[0]()
-    rs_m[1]()
-    ag_h[1]()
-    rs_f[2]()
-    tw_o = twin(R.ob)
-
-    @pl.loop(0, 4)
-    def _(t):
-        rows = owned(t)
-        R.ob[zh, rows] = (R.hid[rows] + rs_f[4](rows)).astype(BF)
-
-    rs_f[3]()
-    tw_o[0]()
-    ag_h[2]()
+    rs2.end()
+    ag_h.s0()
+    rs_d.t3()
+    ag_h.s1()
+    rs_m.onward()
+    ag_h.s2()
+    ag_h.s3()
+    rs_f.s0()
 
     @pl.loop(0, 4)
     def _(i):
         zi, ci = lax.div(i, 2), lax.rem(i, 2)
-        w = R.wa[:, :, :, :, :, PROJ:ATT].reshape(WIDTH, 256)
-        grad = mm(R.nm[i].reshape(128, WIDTH), w)
+        grad = mm(R.nm[i].reshape(128, WIDTH), R.wo[...].reshape(WIDTH, 256))
         logits = jnp.zeros((128, 128), F32)
         for h in (0, 1):
             gate = jax.nn.sigmoid(R.gl[i][:, h : h + 1])
@@ -660,13 +780,15 @@
             R.dox[zi, h, ci, :, 128:256] = three_parts(-delta, lanes)
         R.gsc[i, :, 512:640] = logits.astype(BF)
 
+    rs_d.t4()
+    rs_f.s1()
+
     R.oacc[...] = jnp.zeros((2, 512, 256), F32)
     row_t = lax.broadcasted_iota(jnp.int32, (256, 512), 1)
     key_t = lax.broadcasted_iota(jnp.int32, (256, 512), 0)
     seen_t = key_t <= lax.rem(row_t, 256)
 
-    def backward(t, groups, diagonal):
-        at = tile(t)
+    def backward(at, groups, diagonal):
         k = R.kv[at + (ALL, ALL, slice(0, 128))].reshape(256, 128)
         v = R.kv[at + (ALL, ALL, slice(128, 256))].reshape(256, 128)
         kx = jnp.concatenate([k, ones], axis=1)
@@ -688,28 +810,40 @@
         R.kv[at + (ALL, ALL, slice(0, 128))] = dk.astype(BF).reshape(2, 128, 128)
         R.kv[at + (ALL, ALL, slice(128, 256))] = dv.astype(BF).reshape(2, 128, 128)
 
-    @pl.loop(0, j)
+    def nothing(at):
+        R.kv[at] = jnp.zeros((2, 128, 256), BF)
+
+    rs_k = scatter(R.kv, (R.k_r2, R.k_r1, R.k_q2, R.k_q1), slice(0, 256))
+    side(backward, 2, nothing)
+    rs_k.t0()
+    side(backward, 1, nothing)
+    rs_k.t1(0)
+    rs_m.t3()
+    rs_k.t2(0)
+    rs_f.s2()
+    side(backward, 3, nothing)
+    rs_k.t1(1)
+    rs_k.t2(1)
+    rs_d.t5()
+    R.wm[:, y, x, :, :, 1536:2304] = R.ga[:, y, x, :, :, 0:768]
+    near(backward, nothing)
+    backward((0, y, x), (0, 1), 0)
+    backward((1, y, x), (1,), 1)
+    rs_f.s3()
+    tw_o = twin(R.ob)
+
+    @pl.loop(0, 4)
     def _(t):
-        backward(t, (0, 1), None)
-
-    backward(j, (0, 1), 0)
-    rs_m[2]()
-
-    @pl.loop(j + 1, j + 16)
-    def _(t):
-        backward(t, (1,), None)
-
-    backward(j + 16, (1,), 1)
-
-    @pl.loop(j + 17, 32)
-    def _(t):
-        R.kv[tile(t)] = jnp.zeros((2, 128, 256), BF)
-
-    rs_m[3]()
-    rs_k = scatter(R.kv, (R.k_r2, R.k_r1, R.k_q2, R.k_q1), slice(0, 256))
-    rs_k[0]()
-    rs_m[4]()
-    rs_k[1]()
+        rows = owned(t)
+        R.ob[zh, rows] = (R.hid[rows] + rs_f.total(rows)).astype(BF)
+
+    rs_f.end()
+    tell(group, R.free.at[1])
+    tw_o[0]()
+    rs_m.t4()
+    rs_k.t3()
+    rs_m.t5()
+    tell(ring, R.free.at[2])
     gb_m = give_back(R.wm, R.wlm)
     gb_m[0]()
 
@@ -726,18 +860,23 @@
             R.dgh[0:1, :] += dg
             R.gsc[i, :, h * 128 : (h + 1) * 128] = dv.astype(BF)
 
-    rs_k[2]()
+    rs_k.t4()
 
     @pl.loop(0, 8)
     def _(n):
-        at = (lax.div(n, 4), lax.rem(n, 4), ALL, ALL, ALL, slice(PROJ, ATT))
-        cols = pl.ds(pl.multiple_of(n * 256, 256), 256)
-        t = R.nm[:, :, :, cols].reshape(512, 256).T
-        g = mm(t, R.gated[...].reshape(512, 256))
-        R.wa[at] = g.astype(BF).reshape(4, 2, 32, 256)
-
-    rs_k[3]()
-    rs_k[4]()
+        at = block(n)
+        g = mm(turned(R.nm, n), R.gated[...].reshape(512, 256))
+        R.ga[at + (slice(0, 256),)] = g.astype(BF).reshape(4, 2, 32, 256)
+        t = turned(R.xn, n)
+        g = mm(t, R.gsc[:, :, 0:256].reshape(512, 256))
+        R.ga[at + (slice(256, 512),)] = g.astype(BF).reshape(4, 2, 32, 256)
+        g = mm(t, R.gsc[:, :, 512:640].reshape(512, 128))
+        R.ga[at + (slice(512, 640),)] = g.astype(BF).reshape(4, 2, 32, 128)
+
+    rs_e = scatter(R.ga, big, slice(0, 640))
+    pl.semaphore_wait(R.free.at[2], 4)
+    rs_k.t5()
+    rs_e.start()
 
     @pl.loop(0, 4)
     def _(i):
@@ -751,46 +890,47 @@
 
     @pl.loop(0, 8)
     def _(n):
-        w = R.wa[lax.div(n, 4), lax.rem(n, 4), :, :, :, 0:PROJ].reshape(256, PROJ)
+        w = R.wa[lax.div(n, 4), lax.rem(n, 4)].reshape(256, PROJ)
         cols, v = spread(n, mm_tb(R.gsc[...].reshape(512, PROJ), w))
         R.pb[:, :, :, cols] = v
 
     rs3 = reduce_rows(R.pb, R.rsib, R.rz)
-    rs3[0]()
+    pl.semaphore_wait(R.free.at[1], 4)
+    rs3.s0()
 
     @pl.loop(0, 8)
     def _(n):
-        at = (lax.div(n, 4), lax.rem(n, 4), ALL, ALL, ALL, slice(0, PROJ))
-        cols = pl.ds(pl.multiple_of(n * 256, 256), 256)
-        t = R.xn[:, :, :, cols].reshape(512, 256).T
-        g = mm(t, R.gsc[...].reshape(512, PROJ))
-        R.wa[at] = g.astype(BF).reshape(4, 2, 32, PROJ)
-
-    rs_a = scatter(R.wa, big, slice(0, ATT))
-    rs_a[0]()
-    rs3[1]()
-    rs_a[1]()
-    rs3[2]()
+        g = mm(turned(R.xn, n), R.gsc[:, :, 256:512].reshape(512, 256))
+        R.ga[block(n) + (slice(640, 896),)] = g.astype(BF).reshape(4, 2, 32, 256)
+
+    rs_l = scatter(R.ga, big, slice(640, 896))
+    rs3.s1()
+    rs_l.start()
+    rs_e.onward()
+    rs3.s2()
+    rs_l.onward()
+    rs_e.t3()
+    rs_l.t3()
+    rs3.s3()
     tw_i = twin(R.ib)
 
     @pl.loop(0, 4)
     def _(t):
         rows = owned(t)
         v = R.x[pl.ds(pl.multiple_of(zh * 64 + t * 16, 16), 16), :].astype(F32)
-        dv, dg = rms_back(v, R.ag[...], rs3[4](rows))
+        dv, dg = rms_back(v, R.ag[...], rs3.total(rows))
         R.dgs[0:1, :] += dg
         R.ib[zh, rows] = (R.gh[rows] + dv).astype(BF)
 
-    tw_i[0]()
-    rs3[3]()
+    rs3.end()
 
     for r in range(16):
         R.sums[0, r : r + 1, :] = R.dgs[0:1, r * 128 : (r + 1) * 128]
         R.sums[0, 16 + r : 17 + r, :] = R.dgs[1:2, r * 128 : (r + 1) * 128]
     R.sums[0, 32:40, :] = R.dgh[...]
-    g_z, g_x, g_y, g_c = Group(3), Group(3), Group(3), Group(1)
-
-    def add_up(g, stage, first, devices):
+
+    def add_up(stage, devices):
+        g, first = Group(len(devices)), (0, 7, 10)[stage]
         for i, d in enumerate(devices):
             g.go(R.sums.at[stage], R.came.at[first + i], d, i)
 
@@ -804,43 +944,30 @@
 
         return finish
 
-    fin = add_up(g_z, 0, 0, zdev)
-    rs_a[2]()
+    fin = add_up(0, group + zsib)
+    tw_i[0]()
+    rs_e.t4()
+    rs_l.t4()
     fin()
-    fin = add_up(g_x, 1, 3, xdev)
-    rs_a[3]()
-    fin()
-    fin = add_up(g_y, 2, 6, ydev)
-    rs_a[4]()
-    gb_a = give_back(R.wa, R.wla)
+    fin = add_up(1, xdev)
+    rs_e.t5()
+    rs_l.t5()
+    gb_a = give_back(R.ga, R.wl8)
     gb_a[0]()
     fin()
-    fin = add_up(g_c, 3, 9, [sib])
-
+    fin = add_up(2, ydev)
     gb_m[1]()
-    for i in range(4):
-        at = slice(i * 768, (i + 1) * 768)
-        R.o_fg[:, at] = R.wlm[i, :, 0:768].astype(F32)
-        R.o_fu[:, at] = R.wlm[i, :, 768:1536].astype(F32)
-        R.o_fd[:, at] = R.wlm[i, :, 1536:2304].astype(F32)
+    R.o_fm[...] = R.wlm[...]
     tw_o[1]()
     R.o_out[...] = R.ob[...].reshape(128, WIDTH)
-    fin()
-    R.o_gain[...] = R.sums[4]
     tw_i[1]()
     R.o_in[...] = R.ib[...].reshape(128, WIDTH)
+    fin()
+    R.o_gain[...] = R.sums[3]
     gb_a[1]()
-    gates = jnp.zeros((32, 8), F32)
-    for i in range(4):
-        R.o_q[:, i * 256 : (i + 1) * 256] = R.wla[i, :, 0:256].astype(F32)
-        R.o_k[:, i * 128 : (i + 1) * 128] = R.wla[i, :, 256:384].astype(F32)
-        R.o_v[:, i * 128 : (i + 1) * 128] = R.wla[i, :, 384:512].astype(F32)
-        R.o_o[:, i * 256 : (i + 1) * 256] = R.wla[i, :, 640:896].astype(F32)
-        pick = select(lambda r, q, i=i: (q == r + 2 * i) & (r < 2), (128, 8))
-        gates = gates + mm(R.wla[i, :, 512:640], pick)
-    R.o_g[...] = gates
-    for g in (ag_x, ag_h):
-        g[3]()
+    R.o_fa[...] = R.wl8[...]
+    ag_x[3]()
+    ag_h.end()
     gb_m[2]()
     gb_a[2]()
     assert count[0] == COPIES, count
@@ -855,19 +982,33 @@
     ("o_out", (128, WIDTH), BF),
     ("o_in", (128, WIDTH), BF),
     ("o_gain", (40, 128), F32),
-    ("o_q", (32, 1024), F32),
-    ("o_k", (32, 512), F32),
-    ("o_v", (32, 512), F32),
-    ("o_g", (32, 8), F32),
-    ("o_o", (32, 1024), F32),
-    ("o_fg", (32, 3072), F32),
-    ("o_fu", (32, 3072), F32),
-    ("o_fd", (32, 3072), F32),
+    ("o_fm", (4, 32, 2304), BF),
+    ("o_fa", (4, 32, ATT), BF),
+]
+RESULTS = [
+    ((128, WIDTH), BF),
+    ((128, WIDTH), BF),
+    ((1, 32), F32),
+    ((32, 1024), F32),
+    ((32, 512), F32),
+    ((32, 512), F32),
+    ((32, 8), F32),
+    ((1, 128), F32),
+    ((1, 128), F32),
+    ((32, 1024), F32),
+    ((1, 32), F32),
+    ((32, 3072), F32),
+    ((32, 3072), F32),
+    ((32, 3072), F32),
 ]
 SCRATCH = [
-    ("wla", (4, 32, ATT), BF),
+    ("wla", (4, 32, PROJ), BF),
+    ("wlo", (4, 32, 256), BF),
+    ("wl8", (4, 32, ATT), BF),
     ("wlm", (4, 32, 2304), BF),
-    ("wa", (2, 4, 4, 2, 32, ATT), BF),
+    ("wa", (2, 4, 4, 2, 32, PROJ), BF),
+    ("wo", (2, 4, 4, 2, 32, 256), BF),
+    ("ga", (2, 4, 4, 2, 32, ATT), BF),
     ("wm", (2, 4, 4, 2, 32, 2304), BF),
     ("kv", (2, 4, 4, 2, 128, 256), BF),
     ("xn", (4, 2, 64, WIDTH), BF),
@@ -890,9 +1031,7 @@
     ("pb", (4, 2, 64, WIDTH), BF),
     ("pb2", (4, 2, 64, WIDTH), BF),
     ("rsib", (2, 2, 64, WIDTH), BF),
-    ("rsib2", (2, 2, 64, WIDTH), BF),
     ("rz", (3, 64, WIDTH), BF),
-    ("rz2", (3, 64, WIDTH), BF),
     ("m_r2", (2, 2, 4, 32, 2304), BF),
     ("m_r1", (2, 2, 4, 2, 32, 2304), BF),
     ("m_q2", (2, 2, 1, 32, 2304), BF),
@@ -903,15 +1042,40 @@
     ("k_q1", (2, 2, 1, 2, 128, 256), BF),
     ("ob", (2, 64, WIDTH), BF),
     ("ib", (2, 64, WIDTH), BF),
-    ("sums", (5, 40, 128), F32),
-    ("came", (10, 40, 128), F32),
+    ("sums", (4, 40, 128), F32),
+    ("came", (13, 40, 128), F32),
 ]
-COPIES = 164
+COPIES = 308
 
 
 def kernel(*refs):
     names = INPUTS + [o[0] for o in OUTPUTS] + [v[0] for v in SCRATCH] + ["send", "recv", "free"]
     body(SimpleNamespace(**dict(zip(names, refs))))
+
+
+def finish(out, grad_in, gain, fm, fa, *to):
+    to[0][...] = out[...]
+    to[1][...] = grad_in[...]
+    place = lax.axis_index("seq")
+    for at, first in ((2, 0), (10, 16)):
+        v = gain[pl.ds(first + lax.div(place, 4), 1), :]
+        to[at][...] = pltpu.roll(v, lax.rem(128 - lax.rem(place, 4) * 32, 128), 1)[:, 0:32]
+    to[7][...] = gain[32:33, :]
+    to[8][...] = gain[33:34, :]
+    gates = jnp.zeros((32, 8), F32)
+    for i in range(4):
+        wide = slice(i * 256, (i + 1) * 256)
+        low = slice(i * 128, (i + 1) * 128)
+        to[9][:, wide] = fa[i, :, 0:256].astype(F32)
+        to[3][:, wide] = fa[i, :, 256:512].astype(F32)
+        to[4][:, low] = fa[i, :, 640:768].astype(F32)
+        to[5][:, low] = fa[i, :, 768:896].astype(F32)
+        pick = select(lambda r, q, i=i: (q == r + 2 * i) & (r < 2), (128, 8))
+        gates = gates + mm(fa[i, :, 512:640], pick)
+        for k in range(3):
+            cols = slice(k * 768, (k + 1) * 768)
+            to[11 + k][:, i * 768 : (i + 1) * 768] = fm[i, :, cols].astype(F32)
+    to[6][...] = gates
 
 
 def per_device(
@@ -948,7 +1112,7 @@
         out_specs=[vmem] * len(OUTPUTS),
         scratch_shapes=[pltpu.VMEM(shape, kind) for _, shape, kind in SCRATCH]
         + [pltpu.SemaphoreType.DMA((COPIES,)), pltpu.SemaphoreType.DMA((COPIES,))]
-        + [pltpu.SemaphoreType.REGULAR],
+        + [pltpu.SemaphoreType.REGULAR((3,))],
         compiler_params=pltpu.CompilerParams(
             collective_id=0, has_side_effects=True, vmem_limit_bytes=63 * 2**20
         ),
@@ -971,24 +1135,18 @@
         cos,
         sin,
     )
-    output, grad_inputs, gains, gq, gk, gv, gg, go, gfg, gfu, gfd = out
-    own = lax.dynamic_slice_in_dim(gains[:32].reshape(2, WIDTH), place * 32, 32, 1)
-    return (
-        output,
-        grad_inputs,
-        own[0],
-        gq,
-        gk,
-        gv,
-        gg,
-        gains[32],
-        gains[33],
-        go.T,
-        own[1],
-        gfg,
-        gfu,
-        gfd.T,
-    )
+    out = pl.pallas_call(
+        finish,
+        out_shape=[jax.ShapeDtypeStruct(shape, kind) for shape, kind in RESULTS],
+        compiler_params=pltpu.CompilerParams(vmem_limit_bytes=60 * 2**20),
+        name="results",
+    )(*out)
+    out = list(out)
+    for i in (2, 7, 8, 10):
+        out[i] = out[i].reshape(-1)
+    for i in (9, 13):
+        out[i] = out[i].T
+    return tuple(out)
 
 
 def solution(mesh):

time: 320 us -> 243 us (0.76)
  Pallas kernels: 304 us -> 237 us
  local copies, waits for them, and re-layouts: 12.4 us -> 2.65 us
    pallas_call x1, Pallas kernels: 304 us -> 234 us  [per_device(): pl.pallas_call(kernel, out_shape=[jax.ShapeDtypeStruct(shape, kind) for _...]
    unnamed x33 -> x6, local copies, waits for them, and re-layouts: 11.2 us -> 2.65 us
where the time goes in v2:
time: 243 us
  Pallas kernels  237 us (98%)
  local copies, waits for them, and re-layouts  2.65 us (1%)
    pallas_call x1, Pallas kernels, per_device(): pl.pallas_call(kernel, out_shape=[jax.ShapeDtypeStruct(shape, kind) for _...  234 us

profile of v2, /device:TPU:1, one launch (start us, length us, event | category | flops | bytes accessed | tf_op | source)
XLA Modules:
  0.0 242.6 jit_solution(12399216959737434285)
XLA Ops:
  0.7 0.0 copy-start.1
  0.7 0.1 add_convert_fusion
  0.8 0.6 copy-done.1
  1.4 0.7 copy.28.refs_9_
  2.0 1.0 fusion
  3.0 1.0 pad_maximum_fusion
  4.0 234.1 %block.1 = (bf16[128,2048]{1,0:T(8,128)(2,1)}, bf16[128,2048]{1,0:T(8,128)(2,1)}, f32[40,128]{1,0:T(8,128)}, bf16[4,32,2304]{2,1,0:T(8,128)(2,1)}, bf16[4,32,896]{2,1,0:T(8,128)(2,1)}) custom-call(bf16[128,2048]{1,0:T(8,128)(2,1)} %refs_0_.1, bf16[128,2048]{1,0:T(8,128)(2,1)} %refs_1_.1, f32[1,2048]{1,0:T(1,128)} %bitcast.14, f32[1,128]{1,0:T(1,128)} %bitcast.16, ...), custom_call_target="tpu_custom_call" | custom-call | tf_op jit(solution)/shard_map/block/pallas_call | solution.py:1108
  238.2 3.0 %results.1 = (bf16[128,2048]{1,0:T(8,128)(2,1)}, bf16[128,2048]{1,0:T(8,128)(2,1)}, f32[1,32]{1,0:T(1,128)}, f32[32,1024]{1,0:T(8,128)}, f32[32,512]{1,0:T(8,128...) custom-call(bf16[128,2048]{1,0:T(8,128)(2,1)} %get-tuple-element.33., ...), custom_call_target="tpu_custom_call" | custom-call | tf_op jit(solution)/shard_map/results/pallas_call | solution.py:1138
  241.2 0.0 copy-start
  241.2 0.7 copy-done
  241.9 0.7 copy.29
  (2 shorter events, 0.0 us)
Async XLA Ops:
  0.7 0.7 copy-start.1
  241.2 0.7 copy-start

commit v3 on v2

--- a/solution.py
+++ b/solution.py
@@ -2,6 +2,7 @@
 
 import jax
 import jax.numpy as jnp
+import numpy as np
 from jax import lax
 from jax.experimental import pallas as pl
 from jax.experimental.pallas import tpu as pltpu
@@ -13,7 +14,7 @@
 HEAD = 128
 EIGHTH = 768
 ATT = 896
-PROJ = 640
+PROJ = 512
 SCALE = HEAD**-0.5
 LOG2E = 1.4426950408889634
 LN2 = 0.6931471805599453
@@ -102,8 +103,8 @@
         return count[0] - k
 
     class Group:
-        def __init__(self, k):
-            self.base, self.sent = ids(k), []
+        def __init__(self, k, base=None):
+            self.base, self.sent = ids(k) if base is None else base, []
 
         def copy(self, src, dst, d, i):
             i += self.base
@@ -124,8 +125,8 @@
             for cp in self.sent:
                 cp.wait_send()
 
-    def exchange(buf, wl):
-        g = Group(3)
+    def exchange(buf, wl, base):
+        g = Group(3, base)
 
         def start():
             buf[zl, y, x, c] = wl[me]
@@ -141,8 +142,8 @@
 
         return start, wait, g.end
 
-    def give_back(src, dst):
-        g = Group(3)
+    def give_back(src, dst, base):
+        g = Group(3, base)
 
         def start():
             dst[me] = src[zl, y, x, c]
@@ -174,12 +175,13 @@
         k=1, pos=y, dev=ydev,
     )
 
-    def gather_ring(buf, a):
-        g, p = Group(6), a.pos
+    def gather_ring(buf, a, cs, base):
+        g, p = Group(6, base), a.pos
         left, right, across = up(p, 3), up(p, 1), up(p, 2)
 
         def half(q, h):
-            return buf.at[a.half(q, h)]
+            at = a.half(q, h)
+            return buf.at[at if cs is None else at + (ALL,) * (5 - len(at)) + (cs,)]
 
         def s1():
             for i, (h, d) in enumerate(((0, 0), (1, 1), (1, 0), (0, 1))):
@@ -201,9 +203,9 @@
 
         return s1, s2, s3, s4, g.end
 
-    def gather(buf):
-        one = [gather_ring(buf, a_x), gather_ring(buf, b_y)]
-        two = [gather_ring(buf, a_y), gather_ring(buf, b_x)]
+    def gather(buf, base, cs=None):
+        one = [gather_ring(buf, a_x, cs, base), gather_ring(buf, b_y, cs, base + 6)]
+        two = [gather_ring(buf, a_y, cs, base + 12), gather_ring(buf, b_x, cs, base + 18)]
 
         def t1():
             for r in one:
@@ -235,8 +237,8 @@
 
         return t1, t2, t3, t4, t5, t6
 
-    def reduce_ring(buf, a, r2, r1, cs, bs):
-        g, p, k = Group(6), a.pos, a.k
+    def reduce_ring(buf, a, r2, r1, cs, bs, rows, base):
+        g, p, k = Group(6, base), a.pos, a.k
         first = ALL if k == 4 else 0
 
         def half(q, h):
@@ -247,10 +249,10 @@
             return a.elem(q, n, h) + (ALL, cs)
 
         def far(i):
-            return r2.at[i, first, :, bs]
+            return r2.at[i, first, rows, bs]
 
         def near(i, h):
-            return r1.at[i, first, h, :, bs]
+            return r1.at[i, first, h, rows, bs]
 
         def loop(fn):
             if k == 1:
@@ -271,7 +273,7 @@
 
             def add(n):
                 at = elem(to, n, i)
-                buf[at] = buf[at] + r2[i, n, :, bs]
+                buf[at] = buf[at] + r2[i, n, rows, bs]
 
             loop(add)
             g.go(half(to, i), near(i, i), a.dev[i], 4 + i)
@@ -286,8 +288,8 @@
                     at = elem(p, n, h)
                     total = (
                         buf[at].astype(F32)
-                        + r1[0, n, h, :, bs].astype(F32)
-                        + r1[1, n, h, :, bs].astype(F32)
+                        + r1[0, n, h, rows, bs].astype(F32)
+                        + r1[1, n, h, rows, bs].astype(F32)
                     )
                     buf[at] = total.astype(BF)
 
@@ -295,15 +297,15 @@
 
         return s1, direct, s2, s3, g.end
 
-    def scatter(buf, bufs, cs, bs=None):
+    def scatter(buf, bufs, base, cs, bs=None, rows=ALL):
         bs = cs if bs is None else bs
         one = [
-            reduce_ring(buf, a_y, bufs[0].at[0], bufs[1].at[0], cs, bs),
-            reduce_ring(buf, b_x, bufs[0].at[1], bufs[1].at[1], cs, bs),
+            reduce_ring(buf, a_y, bufs[0].at[0], bufs[1].at[0], cs, bs, rows, base),
+            reduce_ring(buf, b_x, bufs[0].at[1], bufs[1].at[1], cs, bs, rows, base + 6),
         ]
         two = [
-            reduce_ring(buf, a_x, bufs[2].at[0], bufs[3].at[0], cs, bs),
-            reduce_ring(buf, b_y, bufs[2].at[1], bufs[3].at[1], cs, bs),
+            reduce_ring(buf, a_x, bufs[2].at[0], bufs[3].at[0], cs, bs, rows, base + 12),
+            reduce_ring(buf, b_y, bufs[2].at[1], bufs[3].at[1], cs, bs, rows, base + 18),
         ]
 
         def t0():
@@ -352,8 +354,10 @@
 
     half_rows = (slice(0, 32), slice(32, 64))
 
+    rows_base = ids(8)
+
     def reduce_rows(pb, rsib, rz):
-        g = Group(8)
+        g = Group(8, rows_base)
 
         def mine(zz, h):
             return pb.at[place(zz, c) + (half_rows[h],)]
@@ -397,8 +401,10 @@
 
         return SimpleNamespace(s0=s0, s1=s1, s2=s2, s3=s3, end=g.end, total=total)
 
+    spread_base = ids(10)
+
     def gather_rows(buf):
-        g = Group(10)
+        g = Group(10, spread_base)
 
         def at(zz, h):
             return buf.at[place(zz, c) + (half_rows[h],)]
@@ -471,13 +477,16 @@
         R.wla[i, :, 0:256] = R.qw[:, i * 256 : (i + 1) * 256]
         R.wla[i, :, 256:384] = R.kw[:, i * 128 : (i + 1) * 128]
         R.wla[i, :, 384:512] = R.vw[:, i * 128 : (i + 1) * 128]
-        pick = select(lambda r, q, i=i: (r == q + 2 * i) & (q < 2), (8, 128))
-        R.wla[i, :, 512:640] = mm(R.gw[...], pick).astype(BF)
-    ex_a, ex_o, ex_m = exchange(R.wa, R.wla), exchange(R.wo, R.wlo), exchange(R.wm, R.wlm)
-    ag_a, ag_o, ag_m = gather(R.wa), gather(R.wo), gather(R.wm)
+    pairs, rings = [ids(3) for _ in range(3)], [ids(24) for _ in range(5)]
+    ex_a = exchange(R.wa, R.wla, pairs[0])
+    ex_o = exchange(R.wo, R.wlo, pairs[1])
+    ex_m = exchange(R.wm, R.wlm, pairs[2])
+    ag_a, ag_o = gather(R.wa, rings[0]), gather(R.wo, rings[1])
+    ag_m = gather(R.wm, rings[2], slice(0, 1536))
+    ag_d = gather(R.wm, rings[3], slice(1536, 2304))
     ag_x = gather_blocks(R.xn)
     ag_c = gather_blocks(R.cot)
-    ag_kv = gather(R.kv)
+    ag_kv = gather(R.kv, rings[4])
 
     pl.semaphore_wait(barrier, len(greet))
     ex_a[0]()
@@ -489,45 +498,54 @@
         R.xn[me, lax.div(t, 2), rows] = (v * rms_scale(v) * R.ag[...]).astype(BF)
 
     ag_x[0]()
+    first = lax.broadcasted_iota(jnp.int32, (128, 128), 1) < 64
     for i in range(4):
-        R.wlo[i] = R.ow[:, i * 256 : (i + 1) * 256]
+        base = (i // 2) * 32 + j * 2 + i % 2
+        cb, sb = R.cb[pl.ds(base, 1), :], R.sb[pl.ds(base, 1), :]
+        sin = sb * R.cr[...] + cb * R.sr[...]
+        R.cos[i] = cb * R.cr[...] - sb * R.sr[...]
+        R.sin[i] = jnp.where(first, -sin, sin)
+        R.wlo[i, :, 0:256] = R.ow[:, i * 256 : (i + 1) * 256]
+        pick = select(lambda r, q, i=i: (r == q + 2 * i) & (q < 2), (8, 128))
+        R.wlo[i, :, 256:384] = mm(R.gw[...].T, pick).astype(BF)
         R.wlm[i, :, 0:768] = R.fg[:, i * 768 : (i + 1) * 768]
         R.wlm[i, :, 768:1536] = R.fu[:, i * 768 : (i + 1) * 768]
         R.wlm[i, :, 1536:2304] = R.fd[:, i * 768 : (i + 1) * 768]
     R.cot[me] = R.ct[...].reshape(2, 64, WIDTH)
     ex_a[1]()
     ag_a[0]()
+    ex_o[0]()
+    ex_m[0]()
     ag_a[1]()
     ag_x[1]()
     ag_a[2]()
-    ex_o[0]()
-    ex_m[0]()
     ag_x[2]()
     ag_a[3]()
     ex_o[1]()
     ag_o[0]()
-    ag_a[4]()
     ex_m[1]()
     ag_m[0]()
+    ag_d[0]()
+    ag_a[4]()
     ag_a[5]()
 
-    @pl.loop(0, 4)
-    def _(i):
-        zi, ci = lax.div(i, 2), lax.rem(i, 2)
+    @pl.loop(0, 2)
+    def _(zi):
         w = R.wa[...].reshape(WIDTH, PROJ)
-        raw = mm(R.xn[i].reshape(128, WIDTH), w)
-        cos, sin = R.cos[i], R.sin[i]
-        R.qraw[i] = raw[:, 0:256]
-        R.kraw[i] = raw[:, 256:384]
-        R.gl[i] = raw[:, 512:640]
-        for h in (0, 1):
-            v = raw[:, h * 128 : (h + 1) * 128]
-            q = rope(v * rms_scale(v) * R.qg[...], cos, sin) * (SCALE * LOG2E)
-            R.qx[zi, h, ci, :, 0:128] = q.astype(BF)
-        v = raw[:, 256:384]
-        k = rope(v * rms_scale(v) * R.kg[...], cos, sin)
-        R.kv[zi, y, x, ci, :, 0:128] = k.astype(BF)
-        R.kv[zi, y, x, ci, :, 128:256] = raw[:, 384:512].astype(BF)
+        both = mm(R.xn[pl.ds(zi * 2, 2)].reshape(256, WIDTH), w)
+        for ci in (0, 1):
+            i, raw = zi * 2 + ci, both[ci * 128 : (ci + 1) * 128]
+            cos, sin = R.cos[i], R.sin[i]
+            R.qraw[i] = raw[:, 0:256]
+            R.kraw[i] = raw[:, 256:384]
+            for h in (0, 1):
+                v = raw[:, h * 128 : (h + 1) * 128]
+                q = rope(v * rms_scale(v) * R.qg[...], cos, sin) * (SCALE * LOG2E)
+                R.qx[zi, h, ci, :, 0:128] = q.astype(BF)
+            v = raw[:, 256:384]
+            k = rope(v * rms_scale(v) * R.kg[...], cos, sin)
+            R.kv[zi, y, x, ci, :, 0:128] = k.astype(BF)
+            R.kv[zi, y, x, ci, :, 128:256] = raw[:, 384:512].astype(BF)
 
     ag_kv[0]()
     ag_c[0]()
@@ -580,26 +598,34 @@
             tile_pair(fn, empty, (up(y, a), k), (k, up(x, a)))
 
     ag_o[1]()
+    ag_m[1]()
+    ag_d[1]()
     forward((0, y, x), (0, 1), 0)
     forward((1, y, x), (1,), 1)
     ag_kv[1]()
-    ag_m[1]()
     ag_kv[2]()
-    ag_o[2]()
     near(forward)
     ag_c[1]()
     ag_kv[3]()
-    ag_o[3]()
+    ag_o[2]()
     ag_kv[4]()
-    ag_m[2]()
+
     @pl.loop(0, 2)
     def _(k):
         side(forward, 1 + 2 * k)
 
+    ag_o[3]()
+    ag_m[2]()
     ag_kv[5]()
     side(forward, 2)
     ag_o[4]()
     ag_o[5]()
+
+    @pl.loop(0, 2)
+    def _(zi):
+        w = R.wo[:, :, :, :, :, 256:384].reshape(WIDTH, 128)
+        v = mm(R.xn[pl.ds(zi * 2, 2)].reshape(256, WIDTH), w)
+        R.gl[pl.ds(zi * 2, 2)] = v.reshape(2, 128, 128)
 
     lanes = lax.broadcasted_iota(jnp.int32, (128, 128), 1)
 
@@ -625,9 +651,9 @@
     def project(cc):
         rows = jnp.concatenate([R.gated[cc], R.gated[2 + cc]], axis=0)
 
-        @pl.loop(0, 8)
+        @pl.loop(0, 8, unroll=4)
         def _(n):
-            w = R.wo[lax.div(n, 4), lax.rem(n, 4)].reshape(256, 256)
+            w = R.wo[lax.div(n, 4), lax.rem(n, 4), :, :, :, 0:256].reshape(256, 256)
             cols = pl.ds(pl.multiple_of(n * 256, 256), 256)
             v = mm_tb(rows, w).astype(BF).reshape(2, 2, 64, 256)
             R.pb[cc, :, :, cols] = v[0]
@@ -639,6 +665,7 @@
     rs1.s1()
     rs1.s2()
     ag_m[3]()
+    ag_d[2]()
     rs1.s3()
 
     def owned(t):
@@ -658,27 +685,26 @@
     ag_n.s0()
     ag_c[2]()
     ag_n.s1()
+    ag_m[4]()
     ag_n.s2()
-    ag_m[4]()
     ag_m[5]()
+    ag_d[3]()
     ag_n.s3()
 
-    @pl.loop(0, 3)
+    def weight(k, n):
+        at = pl.ds(pl.multiple_of(k * 768 + n * 256, 256), 256)
+        return R.wm[:, :, :, :, :, at].reshape(WIDTH, 256)
+
+    @pl.loop(0, 3, unroll=3)
     def _(n):
         cols = pl.ds(pl.multiple_of(n * 256, 256), 256)
-
-        def weight(k):
-            at = pl.ds(pl.multiple_of(k * 768 + n * 256, 256), 256)
-            return R.wm[:, :, :, :, :, at].reshape(WIDTH, 256)
-
         rows = R.nm[...].reshape(512, WIDTH)
-        gate = mm(rows, weight(0))
-        upper = mm(rows, weight(1))
-        grad = mm(R.cot[...].reshape(512, WIDTH), weight(2))
+        gate = mm(rows, weight(0, n))
+        upper = mm(rows, weight(1, n))
         sg = jax.nn.sigmoid(gate)
         silu = gate * sg
-        R.act[0, :, cols] = (grad * upper * (sg * (1.0 + gate * (1.0 - sg)))).astype(BF)
-        R.act[1, :, cols] = (grad * silu).astype(BF)
+        R.act[0, :, cols] = (upper * (sg * (1.0 + gate * (1.0 - sg)))).astype(BF)
+        R.act[1, :, cols] = silu.astype(BF)
         R.act[2, :, cols] = (silu * upper).astype(BF)
 
     def block(n):
@@ -689,17 +715,26 @@
         return ref[:, :, :, cols].reshape(512, 256).T
 
     big = (R.m_r2, R.m_r1, R.m_q2, R.m_q1)
-    rs_d = scatter(R.ga, big, slice(0, 768))
-    rs_m = scatter(R.wm, big, slice(0, 1536), slice(768, 2304))
-
-    @pl.loop(0, 8)
+    rs_d = scatter(R.ga, big, rings[0], slice(0, 768))
+    rs_m = scatter(R.wm, big, rings[1], slice(0, 1536), slice(768, 2304))
+
+    @pl.loop(0, 8, unroll=4)
     def _(n):
         g = mm(turned(R.cot, n), R.act[2])
         R.ga[block(n) + (slice(0, 768),)] = g.astype(BF).reshape(4, 2, 32, 768)
 
     rs_d.start()
-
-    @pl.loop(0, 8)
+    ag_d[4]()
+    ag_d[5]()
+
+    @pl.loop(0, 3, unroll=3)
+    def _(n):
+        cols = pl.ds(pl.multiple_of(n * 256, 256), 256)
+        grad = mm(R.cot[...].reshape(512, WIDTH), weight(2, n))
+        R.act[0, :, cols] = (grad * R.act[0, :, cols].astype(F32)).astype(BF)
+        R.act[1, :, cols] = (grad * R.act[1, :, cols].astype(F32)).astype(BF)
+
+    @pl.loop(0, 8, unroll=4)
     def _(n):
         at = block(n)
         v = mm_tb(R.act[0], R.wm[at + (slice(0, 768),)].reshape(256, 768))
@@ -717,10 +752,10 @@
         R.wm[at + (slice(0, 768),)] = mm(t, R.act[0]).astype(BF).reshape(4, 2, 32, 768)
         R.wm[at + (slice(768, 1536),)] = mm(t, R.act[1]).astype(BF).reshape(4, 2, 32, 768)
 
-    pl.loop(0, 4)(feed_weights)
+    pl.loop(0, 4, unroll=4)(feed_weights)
     rs2.s1()
     rs_d.onward()
-    pl.loop(4, 8)(feed_weights)
+    pl.loop(4, 8, unroll=4)(feed_weights)
     rs2.s2()
 
     def tell(devices, sem):
@@ -734,7 +769,7 @@
     ag_h = gather_rows(R.nm)
     rs_m.start()
 
-    @pl.loop(0, 8)
+    @pl.loop(0, 8, unroll=4)
     def _(n):
         w = R.wm[block(n) + (slice(1536, 2304),)].reshape(256, 768)
         cols, v = spread(n, mm_tb(R.act[2], w))
@@ -763,22 +798,24 @@
     ag_h.s3()
     rs_f.s0()
 
-    @pl.loop(0, 4)
-    def _(i):
-        zi, ci = lax.div(i, 2), lax.rem(i, 2)
-        grad = mm(R.nm[i].reshape(128, WIDTH), R.wo[...].reshape(WIDTH, 256))
-        logits = jnp.zeros((128, 128), F32)
-        for h in (0, 1):
-            gate = jax.nn.sigmoid(R.gl[i][:, h : h + 1])
-            gr = grad[:, h * 128 : (h + 1) * 128]
-            a = R.att[i, :, h * 128 : (h + 1) * 128]
-            low = (gr * gate).astype(BF)
-            dl = jnp.sum(gr * a, axis=1, keepdims=True) * (gate * (1.0 - gate))
-            logits = jnp.where(lanes == h, dl, logits)
-            delta = jnp.sum(low.astype(F32) * a, axis=1, keepdims=True)
-            R.dox[zi, h, ci, :, 0:128] = low
-            R.dox[zi, h, ci, :, 128:256] = three_parts(-delta, lanes)
-        R.gsc[i, :, 512:640] = logits.astype(BF)
+    @pl.loop(0, 2)
+    def _(zi):
+        w = R.wo[:, :, :, :, :, 0:256].reshape(WIDTH, 256)
+        both = mm(R.nm[pl.ds(zi * 2, 2)].reshape(256, WIDTH), w)
+        for ci in (0, 1):
+            i, grad = zi * 2 + ci, both[ci * 128 : (ci + 1) * 128]
+            logits = jnp.zeros((128, 128), F32)
+            for h in (0, 1):
+                gate = jax.nn.sigmoid(R.gl[i][:, h : h + 1])
+                gr = grad[:, h * 128 : (h + 1) * 128]
+                a = R.att[i, :, h * 128 : (h + 1) * 128]
+                low = (gr * gate).astype(BF)
+                dl = jnp.sum(gr * a, axis=1, keepdims=True) * (gate * (1.0 - gate))
+                logits = jnp.where(lanes == h, dl, logits)
+                delta = jnp.sum(low.astype(F32) * a, axis=1, keepdims=True)
+                R.dox[zi, h, ci, :, 0:128] = low
+                R.dox[zi, h, ci, :, 128:256] = three_parts(-delta, lanes)
+            R.gsc[i, :, 512:640] = logits.astype(BF)
 
     rs_d.t4()
     rs_f.s1()
@@ -813,18 +850,20 @@
     def nothing(at):
         R.kv[at] = jnp.zeros((2, 128, 256), BF)
 
-    rs_k = scatter(R.kv, (R.k_r2, R.k_r1, R.k_q2, R.k_q1), slice(0, 256))
+    small = (R.k_r2, R.k_r1, R.k_q2, R.k_q1)
+    rs_k = scatter(R.kv, small, rings[4], slice(0, 256))
     side(backward, 2, nothing)
     rs_k.t0()
     side(backward, 1, nothing)
     rs_k.t1(0)
-    rs_m.t3()
-    rs_k.t2(0)
-    rs_f.s2()
     side(backward, 3, nothing)
     rs_k.t1(1)
+    rs_f.s2()
+    rs_k.t2(0)
     rs_k.t2(1)
+    rs_m.t3()
     rs_d.t5()
+    tell(ring, R.free.at[2])
     R.wm[:, y, x, :, :, 1536:2304] = R.ga[:, y, x, :, :, 0:768]
     near(backward, nothing)
     backward((0, y, x), (0, 1), 0)
@@ -840,12 +879,6 @@
     rs_f.end()
     tell(group, R.free.at[1])
     tw_o[0]()
-    rs_m.t4()
-    rs_k.t3()
-    rs_m.t5()
-    tell(ring, R.free.at[2])
-    gb_m = give_back(R.wm, R.wlm)
-    gb_m[0]()
 
     R.dgh[...] = jnp.zeros((8, 128), F32)
 
@@ -860,9 +893,9 @@
             R.dgh[0:1, :] += dg
             R.gsc[i, :, h * 128 : (h + 1) * 128] = dv.astype(BF)
 
-    rs_k.t4()
-
-    @pl.loop(0, 8)
+    rs_m.t4()
+
+    @pl.loop(0, 8, unroll=4)
     def _(n):
         at = block(n)
         g = mm(turned(R.nm, n), R.gated[...].reshape(512, 256))
@@ -873,10 +906,15 @@
         g = mm(t, R.gsc[:, :, 512:640].reshape(512, 128))
         R.ga[at + (slice(512, 640),)] = g.astype(BF).reshape(4, 2, 32, 128)
 
-    rs_e = scatter(R.ga, big, slice(0, 640))
+    rs_e = scatter(R.ga, big, rings[2], slice(0, 640))
     pl.semaphore_wait(R.free.at[2], 4)
+    rs_k.t3()
+    rs_m.t5()
+    gb_m = give_back(R.wm, R.wlm, pairs[0])
+    gb_m[0]()
+    rs_k.t4()
+    rs_e.start()
     rs_k.t5()
-    rs_e.start()
 
     @pl.loop(0, 4)
     def _(i):
@@ -888,41 +926,29 @@
         R.gsc[i, :, 256:384] = dv.astype(BF)
         R.gsc[i, :, 384:512] = R.kv[zi, y, x, ci, :, 128:256]
 
-    @pl.loop(0, 8)
+    @pl.loop(0, 8, unroll=4)
     def _(n):
-        w = R.wa[lax.div(n, 4), lax.rem(n, 4)].reshape(256, PROJ)
-        cols, v = spread(n, mm_tb(R.gsc[...].reshape(512, PROJ), w))
+        g = mm(turned(R.xn, n), R.gsc[:, :, 256:512].reshape(512, 256))
+        R.ga[block(n) + (slice(640, 896),)] = g.astype(BF).reshape(4, 2, 32, 256)
+
+    rs_l = scatter(R.ga, small, rings[3], slice(640, 896), slice(0, 256), slice(0, 32))
+    rs_l.start()
+
+    @pl.loop(0, 8, unroll=4)
+    def _(n):
+        at = block(n)
+        v = mm_tb(R.gsc[:, :, 0:512].reshape(512, 512), R.wa[at].reshape(256, PROJ))
+        w = R.wo[at + (slice(256, 384),)].reshape(256, 128)
+        v = v + mm_tb(R.gsc[:, :, 512:640].reshape(512, 128), w)
+        cols = pl.ds(pl.multiple_of(n * 256, 256), 256)
+        dg = jnp.sum(v * R.xn[:, :, :, cols].reshape(512, 256).astype(F32), axis=0, keepdims=True)
+        R.dgs[0:1, cols] = dg / R.ag[:, cols]
+        cols, v = spread(n, v)
         R.pb[:, :, :, cols] = v
 
     rs3 = reduce_rows(R.pb, R.rsib, R.rz)
     pl.semaphore_wait(R.free.at[1], 4)
     rs3.s0()
-
-    @pl.loop(0, 8)
-    def _(n):
-        g = mm(turned(R.xn, n), R.gsc[:, :, 256:512].reshape(512, 256))
-        R.ga[block(n) + (slice(640, 896),)] = g.astype(BF).reshape(4, 2, 32, 256)
-
-    rs_l = scatter(R.ga, big, slice(640, 896))
-    rs3.s1()
-    rs_l.start()
-    rs_e.onward()
-    rs3.s2()
-    rs_l.onward()
-    rs_e.t3()
-    rs_l.t3()
-    rs3.s3()
-    tw_i = twin(R.ib)
-
-    @pl.loop(0, 4)
-    def _(t):
-        rows = owned(t)
-        v = R.x[pl.ds(pl.multiple_of(zh * 64 + t * 16, 16), 16), :].astype(F32)
-        dv, dg = rms_back(v, R.ag[...], rs3.total(rows))
-        R.dgs[0:1, :] += dg
-        R.ib[zh, rows] = (R.gh[rows] + dv).astype(BF)
-
-    rs3.end()
 
     for r in range(16):
         R.sums[0, r : r + 1, :] = R.dgs[0:1, r * 128 : (r + 1) * 128]
@@ -945,27 +971,51 @@
         return finish
 
     fin = add_up(0, group + zsib)
+    rs_e.onward()
+    rs3.s1()
+    rs_l.onward()
+    fin()
+    fin = add_up(1, xdev)
+    rs3.s2()
+    rs_e.t3()
+    fin()
+    fin = add_up(2, ydev)
+    rs_l.t3()
+    rs3.s3()
+    tw_i = twin(R.ib)
+
+    @pl.loop(0, 4)
+    def _(t):
+        rows = owned(t)
+        v = R.x[pl.ds(pl.multiple_of(zh * 64 + t * 16, 16), 16), :].astype(F32)
+        dv, _ = rms_back(v, R.ag[...], rs3.total(rows))
+        R.ib[zh, rows] = (R.gh[rows] + dv).astype(BF)
+
     tw_i[0]()
+    rs3.end()
     rs_e.t4()
     rs_l.t4()
+    def put(i, src, dst):
+        cp = pltpu.make_async_copy(src, dst, R.put.at[i])
+        cp.start()
+        return cp
+
+    gb_m[1]()
+    puts = [put(0, R.wlm, R.o_fm)]
+    tw_o[1]()
+    puts.append(put(1, R.ob, R.o_out))
     fin()
-    fin = add_up(1, xdev)
+    puts.append(put(2, R.sums.at[3], R.o_gain))
     rs_e.t5()
     rs_l.t5()
-    gb_a = give_back(R.ga, R.wl8)
+    gb_a = give_back(R.ga, R.wl8, pairs[1])
     gb_a[0]()
-    fin()
-    fin = add_up(2, ydev)
-    gb_m[1]()
-    R.o_fm[...] = R.wlm[...]
-    tw_o[1]()
-    R.o_out[...] = R.ob[...].reshape(128, WIDTH)
     tw_i[1]()
-    R.o_in[...] = R.ib[...].reshape(128, WIDTH)
-    fin()
-    R.o_gain[...] = R.sums[3]
+    puts.append(put(3, R.ib, R.o_in))
     gb_a[1]()
-    R.o_fa[...] = R.wl8[...]
+    puts.append(put(4, R.wl8, R.o_fa))
+    for cp in puts:
+        cp.wait()
     ag_x[3]()
     ag_h.end()
     gb_m[2]()
@@ -976,11 +1026,11 @@
 INPUTS = [
     *("x", "ct", "ag", "qg", "kg", "fgain"),
     *("qw", "kw", "vw", "gw", "ow", "fg", "fu", "fd"),
-    *("cos", "sin"),
+    *("cr", "sr", "cb", "sb"),
 ]
 OUTPUTS = [
-    ("o_out", (128, WIDTH), BF),
-    ("o_in", (128, WIDTH), BF),
+    ("o_out", (2, 64, WIDTH), BF),
+    ("o_in", (2, 64, WIDTH), BF),
     ("o_gain", (40, 128), F32),
     ("o_fm", (4, 32, 2304), BF),
     ("o_fa", (4, 32, ATT), BF),
@@ -992,7 +1042,7 @@
     ((32, 1024), F32),
     ((32, 512), F32),
     ((32, 512), F32),
-    ((32, 8), F32),
+    ((8, 32), F32),
     ((1, 128), F32),
     ((1, 128), F32),
     ((32, 1024), F32),
@@ -1003,17 +1053,19 @@
 ]
 SCRATCH = [
     ("wla", (4, 32, PROJ), BF),
-    ("wlo", (4, 32, 256), BF),
+    ("wlo", (4, 32, 384), BF),
     ("wl8", (4, 32, ATT), BF),
     ("wlm", (4, 32, 2304), BF),
     ("wa", (2, 4, 4, 2, 32, PROJ), BF),
-    ("wo", (2, 4, 4, 2, 32, 256), BF),
+    ("wo", (2, 4, 4, 2, 32, 384), BF),
     ("ga", (2, 4, 4, 2, 32, ATT), BF),
     ("wm", (2, 4, 4, 2, 32, 2304), BF),
     ("kv", (2, 4, 4, 2, 128, 256), BF),
     ("xn", (4, 2, 64, WIDTH), BF),
     ("cot", (4, 2, 64, WIDTH), BF),
     ("nm", (4, 2, 64, WIDTH), BF),
+    ("cos", (4, 128, 128), F32),
+    ("sin", (4, 128, 128), F32),
     ("qraw", (4, 128, 256), F32),
     ("kraw", (4, 128, 128), F32),
     ("gl", (4, 128, 128), F32),
@@ -1022,7 +1074,7 @@
     ("oacc", (2, 512, 256), F32),
     ("att", (4, 128, 256), F32),
     ("gated", (4, 128, 256), BF),
-    ("gsc", (4, 128, PROJ), BF),
+    ("gsc", (4, 128, 640), BF),
     ("act", (3, 512, 768), BF),
     ("hid", (64, WIDTH), F32),
     ("gh", (64, WIDTH), F32),
@@ -1045,24 +1097,24 @@
     ("sums", (4, 40, 128), F32),
     ("came", (13, 40, 128), F32),
 ]
-COPIES = 308
+COPIES = 172
 
 
 def kernel(*refs):
-    names = INPUTS + [o[0] for o in OUTPUTS] + [v[0] for v in SCRATCH] + ["send", "recv", "free"]
+    names = INPUTS + [o[0] for o in OUTPUTS] + [v[0] for v in SCRATCH] + ["send", "recv", "free", "put"]
     body(SimpleNamespace(**dict(zip(names, refs))))
 
 
 def finish(out, grad_in, gain, fm, fa, *to):
-    to[0][...] = out[...]
-    to[1][...] = grad_in[...]
+    to[0][...] = out[...].reshape(128, WIDTH)
+    to[1][...] = grad_in[...].reshape(128, WIDTH)
     place = lax.axis_index("seq")
     for at, first in ((2, 0), (10, 16)):
         v = gain[pl.ds(first + lax.div(place, 4), 1), :]
         to[at][...] = pltpu.roll(v, lax.rem(128 - lax.rem(place, 4) * 32, 128), 1)[:, 0:32]
     to[7][...] = gain[32:33, :]
     to[8][...] = gain[33:34, :]
-    gates = jnp.zeros((32, 8), F32)
+    gates = jnp.zeros((8, 32), F32)
     for i in range(4):
         wide = slice(i * 256, (i + 1) * 256)
         low = slice(i * 128, (i + 1) * 128)
@@ -1070,12 +1122,20 @@
         to[3][:, wide] = fa[i, :, 256:512].astype(F32)
         to[4][:, low] = fa[i, :, 640:768].astype(F32)
         to[5][:, low] = fa[i, :, 768:896].astype(F32)
-        pick = select(lambda r, q, i=i: (q == r + 2 * i) & (r < 2), (128, 8))
-        gates = gates + mm(fa[i, :, 512:640], pick)
+        pick = select(lambda r, q, i=i: (r == q + 2 * i) & (q < 2), (8, 128))
+        gates = gates + mm_tb(pick, fa[i, :, 512:640])
         for k in range(3):
             cols = slice(k * 768, (k + 1) * 768)
             to[11 + k][:, i * 768 : (i + 1) * 768] = fm[i, :, cols].astype(F32)
     to[6][...] = gates
+
+
+def rope_tables():
+    inverse = ROPE_BASE ** (-np.arange(HEAD // 2) * 2.0 / HEAD)
+    inverse = np.concatenate([inverse, inverse]).astype(np.float32).astype(np.float64)
+    rows = np.arange(128)[:, None] * inverse
+    blocks = np.arange(64)[:, None] * 128 * inverse
+    return [jnp.asarray(f(a), F32) for a in (rows, blocks) for f in (np.cos, np.sin)]
 
 
 def per_device(
@@ -1094,25 +1154,15 @@
     feed_down,
     cotangent,
 ):
-    place = lax.axis_index("seq")
-    run = lax.rem(lax.div(place, 2), 16)
-    half = jnp.arange(4, dtype=jnp.int32)[:, None]
-    row = jnp.arange(128, dtype=jnp.int32)[None, :]
-    positions = (half // 2) * 4096 + run * 256 + (half % 2) * 128 + row
-    inverse = ROPE_BASE ** (-(jnp.arange(HEAD // 2, dtype=F32) * 2.0) / HEAD)
-    angles = positions.astype(F32)[:, :, None] * inverse
-    cos, sin = jnp.cos(angles), jnp.sin(angles)
-    cos = jnp.concatenate([cos, cos], axis=-1)
-    sin = jnp.concatenate([-sin, sin], axis=-1)
     vmem = pl.BlockSpec(memory_space=pltpu.VMEM)
     out = pl.pallas_call(
         kernel,
         out_shape=[jax.ShapeDtypeStruct(shape, kind) for _, shape, kind in OUTPUTS],
         in_specs=[vmem] * len(INPUTS),
-        out_specs=[vmem] * len(OUTPUTS),
+        out_specs=[pl.BlockSpec(memory_space=pl.ANY)] * len(OUTPUTS),
         scratch_shapes=[pltpu.VMEM(shape, kind) for _, shape, kind in SCRATCH]
         + [pltpu.SemaphoreType.DMA((COPIES,)), pltpu.SemaphoreType.DMA((COPIES,))]
-        + [pltpu.SemaphoreType.REGULAR((3,))],
+        + [pltpu.SemaphoreType.REGULAR((3,)), pltpu.SemaphoreType.DMA((5,))],
         compiler_params=pltpu.CompilerParams(
             collective_id=0, has_side_effects=True, vmem_limit_bytes=63 * 2**20
         ),
@@ -1127,13 +1177,12 @@
         query_weight,
         key_matrix,
         value_matrix,
-        gate_weight,
+        gate_weight.T,
         out_weight.T,
         feed_gate,
         feed_up,
         feed_down.T,
-        cos,
-        sin,
+        *rope_tables(),
     )
     out = pl.pallas_call(
         finish,
@@ -1144,7 +1193,7 @@
     out = list(out)
     for i in (2, 7, 8, 10):
         out[i] = out[i].reshape(-1)
-    for i in (9, 13):
+    for i in (6, 9, 13):
         out[i] = out[i].T
     return tuple(out)
 

time: 243 us -> 223 us (0.918)
  Pallas kernels: 237 us -> 222 us
  local copies, waits for them, and re-layouts: 2.65 us -> 0 us
    pallas_call x1, Pallas kernels: 234 us -> 219 us  [per_device(): pl.pallas_call(kernel, out_shape=[jax.ShapeDtypeStruct(shape, kind) for _...]
    unnamed x6 -> x0, local copies, waits for them, and re-layouts: 2.65 us -> none
where the time goes in v3:
time: 223 us
  Pallas kernels  222 us (100%)
    pallas_call x1, Pallas kernels, per_device(): pl.pallas_call(kernel, out_shape=[jax.ShapeDtypeStruct(shape, kind) for _...  219 us

profile of v3, /device:TPU:1, one launch (start us, length us, event | category | flops | bytes accessed | tf_op | source)
XLA Modules:
  0.0 222.8 jit_solution(928305002166282895)
XLA Ops:
  0.7 219.2 %block.1 = (bf16[2,64,2048]{2,1,0:T(8,128)(2,1)}, bf16[2,64,2048]{2,1,0:T(8,128)(2,1)}, f32[40,128]{1,0:T(8,128)}, bf16[4,32,2304]{2,1,0:T(8,128)(2,1)}, bf16[4,32,896]{2,1,0:T(8,128)(2,1)}) custom-call(bf16[128,2048]{1,0:T(8,128)(2,1)} %refs_0_.1, bf16[128,2048]{1,0:T(8,128)(2,1)} %refs_1_.1, f32[1,2048]{1,0:T(1,128)} %bitcast.16, f32[1,128]{1,0:T(1,128)} %bitcast.19, ...), custom_call_target="tpu_custom_call" | custom-call | tf_op jit(solution)/shard_map/block/pallas_call | solution.py:1158
  219.8 3.0 %results.1 = (bf16[128,2048]{1,0:T(8,128)(2,1)}, bf16[128,2048]{1,0:T(8,128)(2,1)}, f32[1,32]{1,0:T(1,128)}, f32[32,1024]{1,0:T(8,128)}, f32[32,512]{1,0:T(8,128...) custom-call(bf16[2,64,2048]{2,1,0:T(8,128)(2,1)} %get-tuple-element., ...), custom_call_target="tpu_custom_call" | custom-call | tf_op jit(solution)/shard_map/results/pallas_call | solution.py:1187
